TPU v7x, 32 devices: a whole 2x2x4 slice. The times are simulated.
32 devices in a mesh: tower: 2 (over core), dp: 16 (over z, y, x).
Axes of the slice: x: 2, y: 2, z: 4, core: 2. Of those that a mesh axis runs over, the one named last changes fastest.
Arguments:
- block_input: bfloat16 [2, 17280, 768], P('tower', 'dp'), may hold values from -6 to 6
- segments: int32 [224, 77], P('dp'), may hold values from 0 to 19, as said below
- caption_ends: int32 [320], P('dp'), may hold values from 15 to 1077, as said below
- pair_flags: int32 [320], replicated, may hold values from 0 to 1, as said below
- attention_gain: float32 [2, 768], P('tower'), may hold values from 0.1 to 1.9
- attention_bias: float32 [2, 768], P('tower'), may hold values from -3 to 3
- triple_weight: bfloat16 [2, 3, 768, 768], P('tower'), may hold values from -0.21875 to 0.21875
- triple_bias: float32 [2, 2, 768], P('tower'), may hold values from -3 to 3
- mixer_weight: bfloat16 [2, 768, 768], P('tower'), may hold values from -1.25 to 1.25
- mixer_bias: float32 [2, 768], P('tower'), may hold values from -3 to 3
- feed_gain: float32 [2, 768], P('tower'), may hold values from 0.1 to 1.9
- feed_bias: float32 [2, 768], P('tower'), may hold values from -3 to 3
- widen_weight: bfloat16 [2, 768, 3072], P('tower'), may hold values from -0.21875 to 0.21875
- widen_bias: float32 [2, 3072], P('tower'), may hold values from -3 to 3
- narrow_weight: bfloat16 [2, 3072, 768], P('tower'), may hold values from -0.15625 to 0.15625
- narrow_bias: float32 [2, 768], P('tower'), may hold values from -3 to 3
- final_gain: float32 [2, 768], P('tower'), may hold values from 0.1 to 1.9
- final_bias: float32 [2, 768], P('tower'), may hold values from -3 to 3
- embed_weight: bfloat16 [2, 768, 512], P('tower'), may hold values from -0.21875 to 0.21875
- logit_scale: float32 [], replicated, may hold values from 3.6 to 4.4
- loss_scale: float32 [], replicated, may hold values from 160 to 640
Outputs:
- mean_loss: float32 [], replicated
- accuracy: float32 [], replicated
- block_input_gradient: float32 [2, 17280, 768], P('tower', 'dp')
- attention_gain_gradient: float32 [2, 768], P('tower', 'dp')
- attention_bias_gradient: float32 [2, 768], P('tower', 'dp')
- triple_weight_gradient: float32 [2, 3, 768, 768], P('tower', None, 'dp')
- triple_bias_gradient: float32 [2, 2, 768], P('tower', None, 'dp')
- mixer_weight_gradient: float32 [2, 768, 768], P('tower', 'dp')
- mixer_bias_gradient: float32 [2, 768], P('tower', 'dp')
- feed_gain_gradient: float32 [2, 768], P('tower', 'dp')
- feed_bias_gradient: float32 [2, 768], P('tower', 'dp')
- widen_weight_gradient: float32 [2, 768, 3072], P('tower', None, 'dp')
- widen_bias_gradient: float32 [2, 3072], P('tower', 'dp')
- narrow_weight_gradient: float32 [2, 3072, 768], P('tower', 'dp')
- narrow_bias_gradient: float32 [2, 768], P('tower', 'dp')
- final_gain_gradient: float32 [2, 768], P('tower', 'dp')
- final_bias_gradient: float32 [2, 768], P('tower', 'dp')
- embed_weight_gradient: float32 [2, 768, 512], P('tower', 'dp')
- logit_scale_gradient: float32 [], replicated
Inputs may be any that keep to these rules, and one draw needn't show every extreme that they name: `segments`: the 14 caption rows of each dp index hold captions 0 to 19 in order, one or two whole captions a row, each of 16 to 77 tokens; caption k of dp index d is pair d * 20 + k. caption_ends[c] is the last position, counted over the 1078 tokens of its dp index, where segments holds c mod 20. `pair_flags`: the last pair is real.
All inputs are finite; a program needn't handle non-finite values.
Results may differ from a plain program's by a relative error of at most 0.024.
Values may be sent and summed in bfloat16 or wider, within the bound.
No kernel may reach another device: no remote copies, remote signals or barrier semaphores. Data moves between devices by JAX's collectives and lax.ppermute only.
A program may use at most 256 MiB of HBM per device.

v0:
```python
from functools import partial

import jax
import jax.numpy as jnp
from jax import lax
from jax.sharding import PartitionSpec as P

D_TXT = 512
MLP_TXT = 2048
HEAD = 64
IMG_TOK = 50
CTX = 77


def from_partner(block, axis, apart):
    count = lax.axis_size(axis)
    route = []
    for low in range(count):
        high = low | 1 << apart
        if high != low and high < count:
            route += [(low, high), (high, low)]
    return lax.ppermute(block, axis, route)


def dot_plain(left, right):
    return jnp.dot(left, right, preferred_element_type=jnp.float32)


def dot_first(left, right):
    return lax.dot_general(
        left, right, (((0,), (0,)), ((), ())), preferred_element_type=jnp.float32
    )


def dot_second(left, right):
    return lax.dot_general(
        left, right, (((1,), (1,)), ((), ())), preferred_element_type=jnp.float32
    )


def layer_norm(stream, norm_gain, norm_offset):
    centre = stream - jnp.mean(stream, axis=-1, keepdims=True)
    invert = lax.rsqrt(jnp.mean(centre * centre, axis=-1, keepdims=True) + 1e-05)
    return centre * invert * norm_gain + norm_offset


def norm_back(stream, norm_gain, upward):
    centre = stream - jnp.mean(stream, axis=-1, keepdims=True)
    invert = lax.rsqrt(jnp.mean(centre * centre, axis=-1, keepdims=True) + 1e-05)
    normed = centre * invert
    scaled = upward * norm_gain
    downward = invert * (
        scaled
        - jnp.mean(scaled, axis=-1, keepdims=True)
        - normed * jnp.mean(scaled * normed, axis=-1, keepdims=True)
    )
    return (downward, jnp.sum(upward * normed, axis=0), jnp.sum(upward, axis=0))


def column_sums(rounded):
    return jnp.sum(rounded.astype(jnp.float32), axis=0)


def fit_shape(array, target_shape):
    return jnp.pad(
        array, [(0, target - actual) for target, actual in zip(target_shape, array.shape)]
    )


def fit_members(members, shapes):
    return tuple(
        (fit_shape(member[None], target_shape) for member, target_shape in zip(members, shapes))
    )


def own_params(params, width, hidden):
    return (
        params[0][0, :width],
        params[1][0, :width],
        params[2][0, :, :width, :width],
        params[3][0, :, :width],
        params[4][0, :width, :width],
        params[5][0, :width],
        params[6][0, :width],
        params[7][0, :width],
        params[8][0, :width, :hidden],
        params[9][0, :hidden],
        params[10][0, :hidden, :width],
        params[11][0, :width],
        params[12][0, :width],
        params[13][0, :width],
        params[14][0, :width],
    )


def attention_scores(query, key_rows, allowed, shaped):
    scores = (
        jnp.einsum(
            "gqhd,gkhd->ghqk",
            query.reshape(shaped),
            key_rows.reshape(shaped),
            preferred_element_type=jnp.float32,
        )
        * 0.125
    )
    return jnp.where(allowed, scores, -1e30)


def tower_forward(stream, params, setup):
    width, heads, hidden, groups, length, allowed, pooling, spreading = setup
    (
        attention_gain,
        attention_bias,
        triple_weight,
        triple_bias,
        mixer_weight,
        mixer_bias,
        feed_gain,
        feed_bias,
        widen_weight,
        widen_bias,
        narrow_weight,
        narrow_bias,
        final_gain,
        final_bias,
        embed_weight,
    ) = params
    tokens = stream.shape[0]
    shaped = (groups, length, heads, HEAD)
    normed_one = layer_norm(stream, attention_gain, attention_bias).astype(jnp.bfloat16)
    query = (dot_plain(normed_one, triple_weight[0]) + triple_bias[0]).astype(jnp.bfloat16)
    key_rows = dot_plain(normed_one, triple_weight[1]).astype(jnp.bfloat16)
    values = (dot_plain(normed_one, triple_weight[2]) + triple_bias[1]).astype(jnp.bfloat16)
    scores = attention_scores(query, key_rows, allowed, shaped)
    row_peak = jnp.max(scores, axis=-1, keepdims=True)
    powers = jnp.exp(scores - row_peak)
    row_total = jnp.sum(powers, axis=-1, keepdims=True)
    log_total = (row_peak + jnp.log(row_total))[..., 0]
    weights_low = (powers / row_total).astype(jnp.bfloat16)
    mixed = (
        jnp.einsum(
            "ghqk,gkhd->gqhd",
            weights_low,
            values.reshape(shaped),
            preferred_element_type=jnp.float32,
        )
        .reshape(tokens, width)
        .astype(jnp.bfloat16)
    )
    middle = stream + dot_plain(mixed, mixer_weight) + mixer_bias
    normed_two = layer_norm(middle, feed_gain, feed_bias).astype(jnp.bfloat16)
    hidden_pre = dot_plain(normed_two, widen_weight) + widen_bias
    activated = (hidden_pre * jax.nn.sigmoid(1.702 * hidden_pre)).astype(jnp.bfloat16)
    output = middle + dot_plain(activated, narrow_weight) + narrow_bias
    pooled = pooling(output)
    normed_three = layer_norm(pooled, final_gain, final_bias).astype(jnp.bfloat16)
    embedded = dot_plain(normed_three, embed_weight)
    unit_rows = (
        embedded * lax.rsqrt(jnp.sum(embedded * embedded, axis=-1, keepdims=True) + 1e-06)
    ).astype(jnp.bfloat16)
    stored = (
        normed_one,
        jnp.stack([query, key_rows, values]),
        log_total.reshape(-1),
        mixed,
        middle,
        normed_two,
        hidden_pre,
        activated,
        pooled,
        normed_three,
        embedded,
    )
    return (unit_rows, stored)


def tower_back_upper(params, setup, stored, grad_unit):
    spreading = setup[7]
    (
        normed_one,
        triple_rows,
        log_total,
        mixed,
        middle,
        normed_two,
        hidden_pre,
        activated,
        pooled,
        normed_three,
        embedded,
    ) = stored
    feed_gain, widen_weight, narrow_weight, final_gain, embed_weight = (
        params[6],
        params[8],
        params[10],
        params[12],
        params[14],
    )
    inv_norm = lax.rsqrt(jnp.sum(embedded * embedded, axis=-1, keepdims=True) + 1e-06)
    along = jnp.sum(embedded * grad_unit, axis=-1, keepdims=True)
    grad_embed = (inv_norm * grad_unit - inv_norm * inv_norm * inv_norm * embedded * along).astype(
        jnp.bfloat16
    )
    grad_embed_weight = dot_first(normed_three, grad_embed)
    grad_three = dot_second(grad_embed, embed_weight)
    grad_pooled, grad_final_gain, grad_final_bias = norm_back(pooled, final_gain, grad_three)
    grad_output = spreading(grad_pooled)
    grad_branch = grad_output.astype(jnp.bfloat16)
    grad_narrow_weight = dot_first(activated, grad_branch)
    grad_narrow_bias = column_sums(grad_branch)
    grad_active = dot_second(grad_branch, narrow_weight)
    sigmoid_part = jax.nn.sigmoid(1.702 * hidden_pre)
    slope = sigmoid_part + 1.702 * hidden_pre * sigmoid_part * (1.0 - sigmoid_part)
    grad_hidden = (grad_active * slope).astype(jnp.bfloat16)
    grad_widen_weight = dot_first(normed_two, grad_hidden)
    grad_widen_bias = column_sums(grad_hidden)
    grad_two = dot_second(grad_hidden, widen_weight)
    grad_norm_two, grad_feed_gain, grad_feed_bias = norm_back(middle, feed_gain, grad_two)
    grad_middle = grad_output + grad_norm_two
    return (
        grad_middle,
        (
            grad_feed_gain,
            grad_feed_bias,
            grad_widen_weight,
            grad_widen_bias,
            grad_narrow_weight,
            grad_narrow_bias,
            grad_final_gain,
            grad_final_bias,
            grad_embed_weight,
        ),
    )


def tower_back_lower(stream, params, setup, stored, grad_middle):
    width, heads, hidden, groups, length, allowed = setup[:6]
    (
        normed_one,
        triple_rows,
        log_total,
        mixed,
        middle,
        normed_two,
        hidden_pre,
        activated,
        pooled,
        normed_three,
        embedded,
    ) = stored
    attention_gain, triple_weight, mixer_weight = (params[0], params[2], params[4])
    tokens = stream.shape[0]
    shaped = (groups, length, heads, HEAD)
    grad_attention = grad_middle.astype(jnp.bfloat16)
    grad_mixer_weight = dot_first(mixed, grad_attention)
    grad_mixer_bias = column_sums(grad_attention)
    grad_mixed = dot_second(grad_attention, mixer_weight).astype(jnp.bfloat16).reshape(shaped)
    query, key_rows, values = (triple_rows[0], triple_rows[1], triple_rows[2])
    scores = attention_scores(query, key_rows, allowed, shaped)
    probs = jnp.exp(scores - log_total[..., None])
    probs_low = probs.astype(jnp.bfloat16)
    grad_values = (
        jnp.einsum("ghqk,gqhd->gkhd", probs_low, grad_mixed, preferred_element_type=jnp.float32)
        .reshape(tokens, width)
        .astype(jnp.bfloat16)
    )
    grad_probs = jnp.einsum(
        "gqhd,gkhd->ghqk", grad_mixed, values.reshape(shaped), preferred_element_type=jnp.float32
    )
    grad_scores = (
        probs * (grad_probs - jnp.sum(grad_probs * probs, axis=-1, keepdims=True))
    ).astype(jnp.bfloat16)
    grad_query = (
        (
            jnp.einsum(
                "ghqk,gkhd->gqhd",
                grad_scores,
                key_rows.reshape(shaped),
                preferred_element_type=jnp.float32,
            )
            * 0.125
        )
        .reshape(tokens, width)
        .astype(jnp.bfloat16)
    )
    grad_keys = (
        (
            jnp.einsum(
                "ghqk,gqhd->gkhd",
                grad_scores,
                query.reshape(shaped),
                preferred_element_type=jnp.float32,
            )
            * 0.125
        )
        .reshape(tokens, width)
        .astype(jnp.bfloat16)
    )
    grad_triple_weight = jnp.stack(
        [
            dot_first(normed_one, grad_query),
            dot_first(normed_one, grad_keys),
            dot_first(normed_one, grad_values),
        ]
    )
    grad_triple_bias = jnp.stack([column_sums(grad_query), column_sums(grad_values)])
    grad_one = (
        dot_second(grad_query, triple_weight[0])
        + dot_second(grad_keys, triple_weight[1])
        + dot_second(grad_values, triple_weight[2])
    )
    grad_norm_one, grad_attention_gain, grad_attention_bias = norm_back(
        stream, attention_gain, grad_one
    )
    grad_stream = grad_middle + grad_norm_one
    return (
        grad_stream,
        (
            grad_attention_gain,
            grad_attention_bias,
            grad_triple_weight,
            grad_triple_bias,
            grad_mixer_weight,
            grad_mixer_bias,
        ),
    )


def body(
    block_input,
    segments,
    caption_ends,
    pair_flags,
    attention_gain,
    attention_bias,
    triple_weight,
    triple_bias,
    mixer_weight,
    mixer_bias,
    feed_gain,
    feed_bias,
    widen_weight,
    widen_bias,
    narrow_weight,
    narrow_bias,
    final_gain,
    final_bias,
    embed_weight,
    logit_scale,
    loss_scale,
):
    params = (
        attention_gain,
        attention_bias,
        triple_weight,
        triple_bias,
        mixer_weight,
        mixer_bias,
        feed_gain,
        feed_bias,
        widen_weight,
        widen_bias,
        narrow_weight,
        narrow_bias,
        final_gain,
        final_bias,
        embed_weight,
    )
    pad_rows = block_input.shape[1]
    full_width = block_input.shape[2]
    full_hidden = widen_weight.shape[2]
    emb_width = embed_weight.shape[2]
    pairs_here = caption_ends.shape[0]
    text_rows = segments.shape[0]
    image_heads = full_width // HEAD
    text_heads = D_TXT // HEAD
    image_tokens = pairs_here * IMG_TOK
    text_tokens = text_rows * CTX
    lse_size = max(pairs_here * image_heads * IMG_TOK, text_rows * text_heads * CTX)
    image_allowed = jnp.ones((1, 1, IMG_TOK, IMG_TOK), dtype=jnp.bool_)

    def image_pool(output):
        return output.reshape(pairs_here, IMG_TOK, full_width)[:, 0]

    def image_spread(grad_pooled):
        rest = jnp.zeros((pairs_here, IMG_TOK - 1, full_width), jnp.float32)
        return jnp.concatenate([grad_pooled[:, None], rest], axis=1).reshape(
            image_tokens, full_width
        )

    positions = lax.iota(jnp.int32, CTX)
    causal = positions[None, :] <= positions[:, None]
    text_allowed = (causal[None] & (segments[:, :, None] == segments[:, None, :]))[:, None]

    def text_pool(output):
        return jnp.take(output, caption_ends, axis=0)

    def text_spread(grad_pooled):
        return jnp.zeros((text_tokens, D_TXT), jnp.float32).at[caption_ends].add(grad_pooled)

    image_setup = (
        full_width,
        image_heads,
        full_hidden,
        pairs_here,
        IMG_TOK,
        image_allowed,
        image_pool,
        image_spread,
    )
    text_setup = (D_TXT, text_heads, MLP_TXT, text_rows, CTX, text_allowed, text_pool, text_spread)
    padded_shapes = (
        (pad_rows, full_width),
        (3, pad_rows, full_width),
        (lse_size,),
        (pad_rows, full_width),
        (pad_rows, full_width),
        (pad_rows, full_width),
        (pad_rows, full_hidden),
        (pad_rows, full_hidden),
        (pairs_here, full_width),
        (pairs_here, full_width),
        (pairs_here, emb_width),
    )

    def run_forward(setup, tokens):
        sliced = own_params(params, setup[0], setup[2])
        stream = block_input[0, :tokens, : setup[0]].astype(jnp.float32)
        unit_rows, stored = tower_forward(stream, sliced, setup)
        return (
            unit_rows,
            tuple(
                (
                    fit_shape(member, target_shape)
                    for member, target_shape in zip(stored, padded_shapes)
                )
            ),
        )

    tower_now = lax.axis_index("tower")
    is_image = tower_now == 0
    unit_rows, stored_all = lax.cond(
        is_image,
        partial(run_forward, image_setup, image_tokens),
        partial(run_forward, text_setup, text_tokens),
    )

    def trimmed(setup, tokens):
        width, heads, hidden, groups, length = setup[:5]
        sizes_now = (
            (tokens, width),
            (3, tokens, width),
            (groups * heads * length,),
            (tokens, width),
            (tokens, width),
            (tokens, width),
            (tokens, hidden),
            (tokens, hidden),
            (pairs_here, width),
            (pairs_here, width),
            (pairs_here, emb_width),
        )
        parts_now = tuple(
            (
                lax.slice(member, (0,) * len(size_now), size_now)
                for member, size_now in zip(stored_all, sizes_now)
            )
        )
        return parts_now[:2] + (parts_now[2].reshape(groups, heads, length),) + parts_now[3:]

    partner = from_partner(unit_rows, "tower", 0)
    factor = jnp.exp(logit_scale)
    live_flags = (pair_flags > 0).astype(jnp.float32)
    live_pairs = jnp.sum(live_flags)
    dev_now = lax.axis_index("dp")
    rows_at = dev_now * pairs_here + lax.iota(jnp.int32, pairs_here)
    others = lax.all_gather(partner, "dp", axis=0, tiled=True)
    logits = dot_second(unit_rows, others) * factor
    all_pairs = logits.shape[1]
    masked = jnp.where(live_flags[None, :] > 0.5, logits, -1e30)
    row_peak = jnp.max(masked, axis=-1, keepdims=True)
    powers = jnp.exp(masked - row_peak)
    row_total = jnp.sum(powers, axis=-1, keepdims=True)
    log_total = row_peak[:, 0] + jnp.log(row_total[:, 0])
    matching = lax.iota(jnp.int32, all_pairs)[None, :] == rows_at[:, None]
    matched = jnp.sum(jnp.where(matching, logits, 0.0), axis=-1)
    row_live = lax.dynamic_slice_in_dim(live_flags, dev_now * pairs_here, pairs_here)
    loss_part = jnp.sum(row_live * (log_total - matched))
    hits_part = jnp.sum(row_live * jnp.exp(matched - log_total))
    row_weight = row_live * (loss_scale / (2.0 * live_pairs))
    grad_logits = (
        (powers / row_total - matching.astype(jnp.float32)) * row_weight[:, None]
    ).astype(jnp.bfloat16)
    scale_part = jnp.sum(grad_logits.astype(jnp.float32) * logits)
    matrices = (grad_logits,)
    matrix = matrices[0]
    grad_own = dot_plain(matrix, others)
    grad_own = grad_own * factor
    back_columns = lax.psum_scatter(
        dot_first(grad_logits, unit_rows) * factor, "dp", scatter_dimension=0, tiled=True
    )
    returned = from_partner(back_columns.astype(jnp.bfloat16), "tower", 0).astype(
        back_columns.dtype
    )
    grad_unit = grad_own + returned
    totals = lax.psum((loss_part, hits_part, scale_part), ("tower", "dp"))
    mean_loss = totals[0] / (2.0 * live_pairs)
    accuracy = totals[1] / (2.0 * live_pairs)
    upper_shapes = (
        (1, full_width),
        (1, full_width),
        (1, full_width, full_hidden),
        (1, full_hidden),
        (1, full_hidden, full_width),
        (1, full_width),
        (1, full_width),
        (1, full_width),
        (1, full_width, emb_width),
    )
    lower_shapes = (
        (1, full_width),
        (1, full_width),
        (1, 3, full_width, full_width),
        (1, 2, full_width),
        (1, full_width, full_width),
        (1, full_width),
    )

    def run_upper(setup, tokens):
        sliced = own_params(params, setup[0], setup[2])
        grad_middle, grads_now = tower_back_upper(sliced, setup, trimmed(setup, tokens), grad_unit)
        return (
            fit_shape(grad_middle, (pad_rows, full_width)),
            fit_members(grads_now, upper_shapes),
        )

    grad_middle_all, upper_grads = lax.cond(
        is_image,
        partial(run_upper, image_setup, image_tokens),
        partial(run_upper, text_setup, text_tokens),
    )

    def run_lower(setup, tokens):
        width = setup[0]
        sliced = own_params(params, width, setup[2])
        stream = block_input[0, :tokens, :width].astype(jnp.float32)
        grad_stream, grads_now = tower_back_lower(
            stream, sliced, setup, trimmed(setup, tokens), grad_middle_all[:tokens, :width]
        )
        return (
            fit_shape(grad_stream[None], (1, pad_rows, full_width)),
            fit_members(grads_now, lower_shapes),
        )

    block_grad, lower_grads = lax.cond(
        is_image,
        partial(run_lower, image_setup, image_tokens),
        partial(run_lower, text_setup, text_tokens),
    )
    merged = (
        lax.psum_scatter(lower_grads[0], "dp", scatter_dimension=1, tiled=True),
        lax.psum_scatter(lower_grads[1], "dp", scatter_dimension=1, tiled=True),
        lax.psum_scatter(lower_grads[2], "dp", scatter_dimension=2, tiled=True),
        lax.psum_scatter(lower_grads[3], "dp", scatter_dimension=2, tiled=True),
        lax.psum_scatter(lower_grads[4], "dp", scatter_dimension=1, tiled=True),
        lax.psum_scatter(lower_grads[5], "dp", scatter_dimension=1, tiled=True),
        lax.psum_scatter(upper_grads[0], "dp", scatter_dimension=1, tiled=True),
        lax.psum_scatter(upper_grads[1], "dp", scatter_dimension=1, tiled=True),
        lax.psum_scatter(upper_grads[2], "dp", scatter_dimension=2, tiled=True),
        lax.psum_scatter(upper_grads[3], "dp", scatter_dimension=1, tiled=True),
        lax.psum_scatter(upper_grads[4], "dp", scatter_dimension=1, tiled=True),
        lax.psum_scatter(upper_grads[5], "dp", scatter_dimension=1, tiled=True),
        lax.psum_scatter(upper_grads[6], "dp", scatter_dimension=1, tiled=True),
        lax.psum_scatter(upper_grads[7], "dp", scatter_dimension=1, tiled=True),
        lax.psum_scatter(upper_grads[8], "dp", scatter_dimension=1, tiled=True),
    )
    lower_grads = merged[:6]
    upper_grads = merged[6:]
    return (
        mean_loss,
        accuracy,
        block_grad,
        lower_grads[0],
        lower_grads[1],
        lower_grads[2],
        lower_grads[3],
        lower_grads[4],
        lower_grads[5],
        upper_grads[0],
        upper_grads[1],
        upper_grads[2],
        upper_grads[3],
        upper_grads[4],
        upper_grads[5],
        upper_grads[6],
        upper_grads[7],
        upper_grads[8],
        totals[2],
    )


def solution(mesh):
    in_specs = (
        P("tower", "dp", None),
        P("dp", None),
        P("dp"),
        P(),
        P("tower", None),
        P("tower", None),
        P("tower", None, None, None),
        P("tower", None, None),
        P("tower", None, None),
        P("tower", None),
        P("tower", None),
        P("tower", None),
        P("tower", None, None),
        P("tower", None),
        P("tower", None, None),
        P("tower", None),
        P("tower", None),
        P("tower", None),
        P("tower", None, None),
        P(),
        P(),
    )
    out_specs = (
        P(),
        P(),
        P("tower", "dp", None),
        P("tower", "dp"),
        P("tower", "dp"),
        P("tower", None, "dp", None),
        P("tower", None, "dp"),
        P("tower", "dp", None),
        P("tower", "dp"),
        P("tower", "dp"),
        P("tower", "dp"),
        P("tower", None, "dp"),
        P("tower", "dp"),
        P("tower", "dp", None),
        P("tower", "dp"),
        P("tower", "dp"),
        P("tower", "dp"),
        P("tower", "dp", None),
        P(),
    )
    return jax.shard_map(body, mesh=mesh, in_specs=in_specs, out_specs=out_specs, check_vma=False)
```

profile of v0, /device:TPU:0, one launch (start us, length us, event | category | flops | bytes accessed | tf_op | source)
XLA Modules:
  0.0 2365.4 jit_solution(13352470674997857741)
XLA Ops:
  8.3 120.9 %conditional.8 = (bf16[1080,768]{1,0:T(8,128)(2,1)}, bf16[3,1080,768]{2,1,0:T(8,128)(2,1)}, f32[12000]{0:T(1024)S(1)}, bf16[1080,768]{0,1:T(8,128)(2,1)}, f32[10...) conditional(s32[]{:T(128)} %convert_element_type.367, ...), branch_computations={%region_0.10_spmd, %region_10.20_spmd} | conditional | flops 14415538176 | bytes 294752352
  33.6 6.2 reshape.608
  39.8 5.8 reshape.609
  49.8 5.7 multiply_reduce_fusion.15
  61.7 4.5 copy.112
  66.3 6.0 convert_element_type.304
  85.6 9.0 multiply_convert_fusion.5
  94.6 6.8 add_add_fusion
  112.0 10.9 pad.111
  122.9 6.1 pad.112
  135.7 47.0 %all-gather = bf16[16,20,512]{2,1,0:T(8,128)(2,1)} all-gather(bf16[1,20,512]{2,1,0:T(8,128)(2,1)} %bitcast.110), channel_id=1, replica_groups=mesh['tower'=2,'dp'=16] {'dp'}, dimensions={0}, use_global_device_ids=true | all-gather | bytes 348160 | tf_op jit(solution)/shard_map/all_gather | solution.py:477
  189.2 43.0 %fusion = f32[24,512]{1,0:T(8,128)S(1)} fusion(f32[320,512]{1,0:T(8,128)} %convolution_multiply_fusion.1), kind=kCustom, calls=%all-reduce-scatter | all-reduce-scatter fusion | flops 196609 | bytes 705024
  242.4 5.6 concatenate.3
  251.3 77.7 %conditional.6 = (f32[1080,768]{1,0:T(8,128)}, f32[1,768]{1,0:T(1,128)S(1)}, f32[1,768]{1,0:T(1,128)S(1)}, f32[1,768,3072]{1,2,0:T(8,128)}, f32[1,3072]{1,0:T(1,...) conditional(s32[]{:T(128)} %convert_element_type.367, ...), branch_computations={%region_29.47_spmd, %region_47.64_spmd} | conditional | flops 18961514496 | bytes 145157776 | solution.py:537
  277.4 11.8 convert_reduce_fusion.8
  289.3 9.4 multiply_reduce_fusion.19
  298.8 7.8 convolution_bitcast_fusion.6
  316.4 10.4 fusion.194
  335.0 147.2 %conditional.7 = (f32[1,1080,768]{2,1,0:T(8,128)}, f32[1,768]{1,0:T(1,128)S(1)}, f32[1,768]{1,0:T(1,128)S(1)}, f32[1,3,768,768]{2,3,1,0:T(8,128)}, f32[1,2,768]{...) conditional(s32[]{:T(128)} %convert_element_type.367, (f32[1080,768]{1,0:T(8,128)}, ...), branch_computations={%region_64.75_spmd, %region_75.86_spmd} | conditional | flops 9861861376 | bytes 253002688 | solution.py:555
  350.3 5.3 convolution_bitcast_fusion.8
  367.3 5.8 squeeze.114
  373.2 5.8 squeeze.115
  383.1 5.7 fusion.229
  388.9 10.5 multiply_reduce_fusion.29
  403.5 6.2 multiply_convert_fusion.10
  418.0 4.6 copy.139
  422.6 6.2 convert_element_type.351
  440.2 6.3 convert_element_type.348
  450.9 4.5 fusion.241
  458.0 6.0 convert_element_type.355
  464.0 5.9 fusion.224
  491.8 8.1 copy.153
  500.6 9.7 copy.154
  513.1 40.0 %all-reduce.39 = (f32[]{:T(128)}, f32[]{:T(128)}, f32[]{:T(128)}) all-reduce(f32[]{:T(128)} %get-tuple-element.454, f32[]{:T(128)} %get-tuple-element.453, f32[]{:T(128)} %get-tuple-element.451), channel_id=1, replica_groups=mesh['tower'=2,'dp'=16] {'tower','dp'}, use_global_device_ids=true, to_apply=%region_24.25 | all-reduce | flops 3 | bytes 24 | tf_op jit(solution)/shard_map/psum | solution.py:506
  555.7 21.9 reduce-scatter.58.cloned.1.call-done
  579.0 124.0 %reduce-scatter.62.cloned.1.call-done = f32[48,1]{1,0:T(8,128)} async-done(((f32[768,1]{1,0:T(8,128)}), f32[48,1]{1,0:T(8,128)}) %reduce-scatter.62.cloned.1.call-update) | async-done | bytes 208
  704.3 124.6 %reduce-scatter.64.cloned.1.call-done = f32[48,1]{1,0:T(8,128)} async-done(((f32[768,1]{1,0:T(8,128)}), f32[48,1]{1,0:T(8,128)}) %reduce-scatter.64.cloned.1.call-update) | async-done | bytes 208
  830.3 123.9 %reduce-scatter.66.cloned.1.call-done = f32[48,1]{1,0:T(8,128)} async-done(((f32[768,1]{1,0:T(8,128)}), f32[48,1]{1,0:T(8,128)}) %reduce-scatter.66.cloned.1.call-update) | async-done | bytes 208
  955.5 124.6 %reduce-scatter.48.cloned.1.call-done = f32[48,1]{1,0:T(8,128)} async-done(((f32[768,1]{1,0:T(8,128)}), f32[48,1]{1,0:T(8,128)}) %reduce-scatter.48.cloned.1.call-update) | async-done | bytes 208
  1081.4 124.1 %reduce-scatter.50.cloned.1.call-done = f32[48,1]{1,0:T(8,128)} async-done(((f32[768,1]{1,0:T(8,128)}), f32[48,1]{1,0:T(8,128)}) %reduce-scatter.50.cloned.1.call-update) | async-done | bytes 208
  1206.8 124.8 %reduce-scatter.54.cloned.1.call-done = f32[48,1]{1,0:T(8,128)} async-done(((f32[768,1]{1,0:T(8,128)}), f32[48,1]{1,0:T(8,128)}) %reduce-scatter.54.cloned.1.call-update) | async-done | bytes 208
  1332.9 124.0 %reduce-scatter.52.cloned.1.call-done = f32[48,2]{1,0:T(8,128)} async-done(((f32[768,2]{1,0:T(8,128)}), f32[48,2]{1,0:T(8,128)}) %reduce-scatter.52.cloned.1.call-update) | async-done | bytes 400
  1458.3 127.7 %reduce-scatter.60.cloned.1.call-done = f32[192,1]{1,0:T(8,128)} async-done(((f32[3072,1]{1,0:T(8,128)}), f32[192,1]{1,0:T(8,128)}) %reduce-scatter.60.cloned.1.call-update) | async-done | bytes 784
  1587.5 128.1 %reduce-scatter.46.cloned.1.call-done = f32[1,48,512]{2,1,0:T(8,128)} async-done(((f32[1,768,512]{2,1,0:T(8,128)}), f32[1,48,512]{2,1,0:T(8,128)}) %reduce-scatter.46.cloned.1.call-update) | async-done | bytes 98320 | tf_op jit(solution)/shard_map/reduce_scatter | solution.py:575
  1715.6 132.8 %reduce-scatter.40.cloned.1.call-done = f32[1,48,768]{2,1,0:T(8,128)} async-done(((f32[1,768,768]{2,1,0:T(8,128)}), f32[1,48,768]{2,1,0:T(8,128)}) %reduce-scatter.40.cloned.1.call-update) | async-done | bytes 147472 | tf_op jit(solution)/shard_map/reduce_scatter | solution.py:565
  1848.3 155.5 %reduce-scatter.38.cloned.1.call-done = f32[1,3,48,768]{3,2,1,0:T(8,128)} async-done(((f32[1,3,768,768]{3,2,1,0:T(8,128)}), f32[1,3,48,768]{3,2,1,0:T(8,128)}) %reduce-scatter.38.cloned.1.call-update) | async-done | bytes 442384 | tf_op jit(solution)/shard_map/reduce_scatter | solution.py:563
  2003.8 176.0 %reduce-scatter.42.cloned.1.call-done = f32[1,768,192]{1,2,0:T(8,128)} async-done(((f32[1,768,3072]{1,2,0:T(8,128)}), f32[1,768,192]{1,2,0:T(8,128)}) %reduce-scatter.42.cloned.1.call-update) | async-done | bytes 589840 | tf_op jit(solution)/shard_map/reduce_scatter | solution.py:569
  2179.8 176.3 %reduce-scatter.44.cloned.1.call-done = f32[1,192,768]{2,1,0:T(8,128)} async-done(((f32[1,3072,768]{2,1,0:T(8,128)}), f32[1,192,768]{2,1,0:T(8,128)}) %reduce-scatter.44.cloned.1.call-update) | async-done | bytes 589840 | tf_op jit(solution)/shard_map/reduce_scatter | solution.py:571
  (294 shorter events, 203.2 us)
Async XLA Ops:
  7.2 547.2 %reduce-scatter.56.cloned.1.call-start = ((), (), s32[]{:S(2)}) async-start(), calls=%async_computation.24 | async-start | bytes 417792
  13.2 9.4 copy-start.69
  13.2 9.5 copy-start.2
  25.8 19.8 copy-start.16
  80.5 5.2 slice-start
  82.8 11.9 slice-start.2
  85.6 9.0 slice-start.3
  94.6 6.8 copy-start.15
  129.2 55.3 %copy-start.55 = (bf16[20,768]{1,0:T(8,128)(2,1)}, bf16[20,768]{1,0:T(8,128)(2,1)S(1)}, u32[]{:S(2)}) copy-start(bf16[20,768]{1,0:T(8,128)(2,1)S(1)} %get-tuple-element.323) | copy-start | bytes 92164
  129.2 57.5 %copy-start.52 = (f32[12000]{0:T(1024)}, f32[12000]{0:T(1024)S(1)}, u32[]{:S(2)}) copy-start(f32[12000]{0:T(1024)S(1)} %get-tuple-element.326) | copy-start | bytes 144004
  129.2 122.1 %copy-start.65 = (f32[1,768]{1,0:T(1,128)S(1)}, f32[1,768]{1,0:T(1,128)}, u32[]{:S(2)}) copy-start(f32[1,768]{1,0:T(1,128)} %param.37) | copy-start | bytes 9220
  129.2 122.1 %copy-start.66 = (f32[1,768]{1,0:T(1,128)S(1)}, f32[1,768]{1,0:T(1,128)}, u32[]{:S(2)}) copy-start(f32[1,768]{1,0:T(1,128)} %param.43) | copy-start | bytes 9220
  129.2 6.4 collective-permute-start
  185.8 65.5 %copy-start.50 = (f32[20,320]{1,0:T(8,128)}, f32[20,320]{1,0:T(8,128)S(1)}, u32[]{:S(2)}) copy-start(f32[20,320]{1,0:T(8,128)S(1)} %get-tuple-element.533) | copy-start | bytes 76804
  232.8 9.6 collective-permute-start.3
  234.7 7.7 collective-permute-start.2
  238.6 3.8 collective-permute-start.4
  248.7 1.3 collective-permute-start.1
  265.0 5.9 copy-start.57
  289.3 9.5 copy-start.43
  298.8 7.9 copy-start.58
  329.1 5.9 copy-start.63
  329.1 5.9 copy-start
  329.1 5.9 copy-start.53
  329.1 5.9 copy-start.67
  330.1 247.5 %reduce-scatter.58.cloned.1.call-start = ((), (), s32[]{:S(2)}) async-start(), calls=%async_computation.25 | async-start | bytes 417792
  331.1 371.9 %reduce-scatter.62.cloned.1.call-start = ((), (), s32[]{:S(2)}) async-start(), calls=%async_computation.27 | async-start | bytes 417792
  332.8 496.1 %reduce-scatter.64.cloned.1.call-start = ((), (), s32[]{:S(2)}) async-start(), calls=%async_computation.28 | async-start | bytes 417792
  333.9 620.3 %reduce-scatter.66.cloned.1.call-start = ((), (), s32[]{:S(2)}) async-start(), calls=%async_computation.29 | async-start | bytes 417792
  334.9 745.1 %reduce-scatter.48.cloned.1.call-start = ((), (), s32[]{:S(2)}) async-start(), calls=%async_computation.20 | async-start | bytes 417792
  350.3 5.3 copy-start.60
  383.1 5.7 copy-start.6
  388.8 10.5 copy-start.3
  403.5 6.2 copy-start.7
  422.6 6.2 copy-start.41
  428.7 4.4 copy-start.45
  433.2 4.5 copy-start.31
  450.9 4.5 copy-start.10
  464.0 5.9 copy-start.44
  483.2 722.3 %reduce-scatter.50.cloned.1.call-start = ((), (), s32[]{:S(2)}) async-start(), calls=%async_computation.21 | async-start | bytes 417792
  484.2 847.3 %reduce-scatter.54.cloned.1.call-start = ((), (), s32[]{:S(2)}) async-start(), calls=%async_computation.23 | async-start | bytes 417792
  485.3 971.6 %reduce-scatter.52.cloned.1.call-start = ((), (), s32[]{:S(2)}) async-start(), calls=%async_computation.22 | async-start | bytes 417792
  486.3 1099.6 %reduce-scatter.60.cloned.1.call-start = ((), (), s32[]{:S(2)}) async-start(), calls=%async_computation.26 | async-start | bytes 1671168
  488.1 1227.5 %reduce-scatter.46.cloned.1.call-start = ((), (), s32[]{:S(2)}) async-start(), calls=%async_computation.19 | async-start | bytes 1671168 | tf_op jit(solution)/shard_map/reduce_scatter | solution.py:575
  491.2 1357.1 %reduce-scatter.40.cloned.1.call-start = ((), (), s32[]{:S(2)}) async-start(), calls=%async_computation.16 | async-start | bytes 2506752 | tf_op jit(solution)/shard_map/reduce_scatter | solution.py:565
  491.8 1512.0 %reduce-scatter.38.cloned.1.call-start = ((), (), s32[]{:S(2)}) async-start(), calls=%async_computation.15 | async-start | bytes 7520256 | tf_op jit(solution)/shard_map/reduce_scatter | solution.py:563
  500.0 1679.9 %reduce-scatter.42.cloned.1.call-start = ((), (), s32[]{:S(2)}) async-start(), calls=%async_computation.17 | async-start | bytes 10027008 | tf_op jit(solution)/shard_map/reduce_scatter | solution.py:569
  500.5 1855.6 %reduce-scatter.44.cloned.1.call-start = ((), (), s32[]{:S(2)}) async-start(), calls=%async_computation.18 | async-start | bytes 10027008 | tf_op jit(solution)/shard_map/reduce_scatter | solution.py:571
  (26 other events, 52.1 us)
Sparse Core Ops, SparseCore 0:
  330.2 121.3 reduce-scatter.55
  456.9 120.6 reduce-scatter.57
  582.3 120.6 reduce-scatter.61
  708.2 120.7 reduce-scatter.63
  833.5 120.6 reduce-scatter.65
  959.4 120.6 reduce-scatter.47
  1084.7 120.7 reduce-scatter.49
  1210.8 120.6 reduce-scatter.53
  1336.2 120.6 reduce-scatter.51
  1462.3 123.6 reduce-scatter.59
  1592.1 123.4 reduce-scatter.45
  1721.7 126.6 reduce-scatter.39
  1854.2 149.5 reduce-scatter.37
  2009.9 169.8 reduce-scatter.41
  2186.9 169.2 reduce-scatter.43
where the time goes:
time: 2370 us
  waiting for transfers between devices  1790 us (76%)
  local copies, waits for them, and re-layouts  189 us (8%)
  matrix products  147 us (6%)
  blocking collectives  130 us (5%)
  other arithmetic  53.5 us (2%)
  loops' own time  26.3 us (1%)
    unnamed x28, waiting for transfers between devices  1020 us
    reduce_scatter x1, waiting for transfers between devices, body(): lax.psum_scatter(upper_grads[4], 'dp', scatter_dimension=1, tiled=True)  176 us
    reduce_scatter x1, waiting for transfers between devices, body(): lax.psum_scatter(upper_grads[2], 'dp', scatter_dimension=2, tiled=True)  176 us
    reduce_scatter x1, waiting for transfers between devices, body(): lax.psum_scatter(lower_grads[2], 'dp', scatter_dimension=2, tiled=True)  155 us
    reduce_scatter x1, waiting for transfers between devices, body(): lax.psum_scatter(lower_grads[4], 'dp', scatter_dimension=1, tiled=True)  133 us
    reduce_scatter x1, waiting for transfers between devices, body(): lax.psum_scatter(upper_grads[8], 'dp', scatter_dimension=1, tiled=True)  128 us
  transfers between devices with their start and end apart: 20, of which 15 were waited for; matrix products, arithmetic and copies ran while one was open for 8% of the time, Pallas kernels for 0%

commit v1 on v0

v1 whole, which is shorter than its diff:
```python
from functools import partial

import jax
import jax.numpy as jnp
from jax import lax
from jax.experimental import pallas as pl
from jax.experimental.pallas import tpu as pltpu
from jax.sharding import PartitionSpec as P

D_TXT = 512
MLP_TXT = 2048
HEAD = 64
IMG_TOK = 50
CTX = 77
F32 = jnp.float32
BF16 = jnp.bfloat16
VMEM_LIMIT = 60 * 1024 * 1024
CHUNK = 1024
NORM_ROWS = 272
PROJECT_ROWS = 1088
WINDOW = 256


def dot_dims(left, right, left_dim, right_dim, precision=None):
    return lax.dot_general(
        left,
        right,
        (((left_dim,), (right_dim,)), ((), ())),
        preferred_element_type=F32,
        precision=precision,
    )


def mm(left, right):
    return dot_dims(left, right, 1, 0)


def mm_nt(left, right):
    return dot_dims(left, right, 1, 1)


def mm_tn(left, right):
    return dot_dims(left, right, 0, 0)


def iota(shape, dim):
    return lax.broadcasted_iota(jnp.int32, shape, dim)


def sigmoid(rows):
    return 1.0 / (1.0 + jnp.exp(-rows))


def one_hot(condition):
    return condition.astype(F32).astype(BF16)


def normed(rows, mask, width):
    mean = jnp.sum(rows * mask, axis=-1, keepdims=True) / width
    centre = (rows - mean) * mask
    invert = lax.rsqrt(jnp.sum(centre * centre, axis=-1, keepdims=True) / width + 1e-05)
    return centre * invert, invert


def norm_back(rows_hat, invert, gain, upward, mask, width):
    scaled = upward * gain
    mean = jnp.sum(scaled, axis=-1, keepdims=True) / width
    along = jnp.sum(scaled * rows_hat, axis=-1, keepdims=True) / width
    return invert * (scaled - mean * mask - rows_hat * along)


def sums_of(rows):
    return jnp.sum(rows, axis=0, keepdims=True)


def head_mask(rows, pairs, width):
    row = iota((rows, width), 0)
    first = lax.shift_right_logical(iota((rows, width), 1), 6) * pairs
    return (row >= first) & (row < first + pairs)


def repeat_rows(rows, pairs):
    row = iota((rows, pairs), 0)
    return one_hot(lax.rem(row, pairs) == iota((rows, pairs), 1))


def tower_sizes(full_width, full_hidden):
    is_text = lax.axis_index("tower") != 0
    width = jnp.where(is_text, D_TXT, full_width)
    mask = (iota((1, full_width), 1) < width).astype(F32)
    return is_text, width.astype(F32), mask


def fetch(source, target, semaphore):
    copy = pltpu.make_async_copy(source, target, semaphore)
    copy.start()
    return copy


def three_parts(rows):
    parts = []
    for _ in range(3):
        part = rows.astype(BF16).astype(F32)
        parts.append(part)
        rows = rows - part
    return jnp.concatenate(parts, axis=0).astype(BF16)


def over_tokens(tokens, size, step):
    for at in range(0, tokens, size):
        step(at, min(size, tokens - at))


def across(lane_sums, full_width):
    return jnp.concatenate([lane_sums] * (full_width // 128), axis=1)


def pooled_spots(ends_ref, is_text, pairs, copies):
    pair = lax.rem(iota((copies * pairs, pairs), 0), pairs)
    ends = jnp.where(pair == iota((copies * pairs, pairs), 1), ends_ref[...], 0).astype(F32)
    ends = jnp.sum(ends, axis=1, keepdims=True)
    firsts = (lax.rem(iota((copies * pairs, 1), 0), pairs) * IMG_TOK).astype(F32)
    return jnp.where(is_text, ends, firsts)


def embed_back(embedded, grad_unit):
    inv_norm = lax.rsqrt(jnp.sum(embedded * embedded, axis=-1, keepdims=True) + 1e-06)
    along = jnp.sum(embedded * grad_unit, axis=-1, keepdims=True)
    return (inv_norm * grad_unit - inv_norm * inv_norm * inv_norm * embedded * along).astype(BF16)


class Hidden:
    def __init__(self, widen_hbm, narrow_hbm, s_widen, s_narrow, sems, chunks):
        self.pairs = (
            (lambda at: widen_hbm.at[0, :, pl.ds(at, CHUNK)], lambda at: s_widen.at[:, pl.ds(at, CHUNK)]),
            (lambda at: narrow_hbm.at[0, pl.ds(at, CHUNK), :], lambda at: s_narrow.at[pl.ds(at, CHUNK), :]),
        )
        self.sems = sems
        self.chunks = chunks

    def copy(self, which, chunk):
        source, target = self.pairs[which]
        at = chunk * CHUNK
        return pltpu.make_async_copy(source(at), target(at), self.sems.at[which, chunk])

    def start(self, order):
        for chunk in range(self.chunks):
            for which in order:
                self.copy(which, chunk).start()

    def each(self, step):
        for chunk in range(self.chunks):
            self.copy(0, chunk).wait()
            self.copy(1, chunk).wait()
            step(slice(chunk * CHUNK, (chunk + 1) * CHUNK))


def attend_kernel(
    dims,
    ends_ref,
    x_hbm,
    ag,
    ab,
    triple_hbm,
    triple_bias,
    wo_hbm,
    bo,
    fg,
    fb,
    ww_hbm,
    bw,
    wn_hbm,
    bn,
    lg,
    lb,
    we_hbm,
    unit_ref,
    early_ref,
    hat_hbm,
    inv_hbm,
    probs_hbm,
    keys_ref,
    embedded_ref,
    pooled_ref,
    middle_ref,
    slope_ref,
    hat_rows_ref,
    s_x,
    s_one,
    s_hat,
    s_inv,
    s_probs,
    s_key,
    s_value,
    s_triple,
    s_wo,
    s_ww,
    s_wn,
    s_we,
    s_low,
    sems,
    hidden_sems,
):
    pairs, tokens, full_width, full_hidden = dims
    is_text, width, mask = tower_sizes(full_width, full_hidden)
    rows = full_width // HEAD * pairs
    get_x = fetch(x_hbm.at[0], s_x, sems.at[0])
    get_triple = fetch(triple_hbm.at[0], s_triple, sems.at[1])
    gain, shift = ag[...] * mask, ab[...] * mask
    ones = one_hot((iota((full_width, 128), 0)).astype(F32) < width)
    hidden = Hidden(ww_hbm, wn_hbm, s_ww, s_wn, hidden_sems, full_hidden // CHUNK)
    get_x.wait()
    get_wo = fetch(wo_hbm.at[0], s_wo, sems.at[2])
    hidden.start((0, 1))
    get_we = fetch(we_hbm.at[0], s_we, sems.at[3])

    def norm_rows(at, count):
        here = pl.ds(at, count)
        low = s_x[here, :]
        mean = mm(low, ones) / width
        centre = (low.astype(F32) - across(mean, full_width)) * mask
        square = centre * centre
        high = square.astype(BF16)
        low = (square - high.astype(F32)).astype(BF16)
        invert = lax.rsqrt((mm(high, ones) + mm(low, ones)) / width + 1e-05)
        hat = centre * across(invert, full_width)
        s_hat[here, :] = hat.astype(BF16)
        s_one[here, :] = (hat * gain + shift).astype(BF16)
        s_inv[here, :] = invert

    over_tokens(tokens, NORM_ROWS, norm_rows)
    put_hat = fetch(s_hat, hat_hbm, sems.at[4])
    put_inv = fetch(s_inv, inv_hbm, sems.at[5])
    pick = one_hot(iota((pairs, tokens), 1).astype(F32) == pooled_spots(ends_ref, is_text, pairs, 1))
    stream_rows = mm(pick, s_x[...]) * mask
    one = mm(pick, s_one[...]).astype(BF16)
    get_triple.wait()
    query = ((mm(one, s_triple[0]) + triple_bias[0, 0:1, :]) * (mask * 0.125)).astype(BF16)
    repeat = repeat_rows(rows, pairs)
    heads = head_mask(rows, pairs, full_width)
    wide = jnp.where(heads, mm(repeat, query), 0.0).astype(BF16)

    def project(at, count):
        here = pl.ds(at, count)
        s_key[here, :] = mm(s_one[here, :], s_triple[1]).astype(BF16)
        s_value[here, :] = (mm(s_one[here, :], s_triple[2]) + triple_bias[0, 1:2, :]).astype(BF16)

    over_tokens(tokens, PROJECT_ROWS, project)
    s_probs[...] = mm_nt(wide, s_key[...])
    last = pooled_spots(ends_ref, is_text, pairs, rows // pairs)
    pair = lax.rem(iota((rows, 1), 0), pairs)
    stops = jnp.where(
        pair - 1 == iota((rows, pairs), 1), ends_ref[...] + 1, 0
    ).astype(F32)
    first = jnp.where(is_text, jnp.sum(stops, axis=1, keepdims=True), last)
    last = jnp.where(is_text, last, last + (IMG_TOK - 1.0))
    step_rows = 48
    for at in range(0, rows, step_rows):
        here = slice(at, at + step_rows)
        place = iota((step_rows, tokens), 1).astype(F32)
        allowed = (place >= first[here]) & (place <= last[here])
        scores = jnp.where(allowed, s_probs[here, :], -1e30)
        powers = jnp.exp(scores - jnp.max(scores, axis=1, keepdims=True))
        probs = powers * (1.0 / jnp.sum(powers, axis=1, keepdims=True))
        s_probs[here, :] = probs
        s_low[here, :] = probs.astype(BF16)
    put_probs = fetch(s_probs, probs_hbm, sems.at[6])
    mixed_wide = mm(s_low[...], s_value[...])
    mixed = mm_tn(repeat, jnp.where(heads, mixed_wide, 0.0).astype(BF16))
    mixed = (mixed * mask).astype(BF16)
    early_ref[:, 0:full_width] = mixed
    early_ref[:, full_width : 2 * full_width] = stream_rows.astype(BF16)
    get_wo.wait()
    middle = stream_rows + mm(mixed, s_wo[...]) + bo[...]
    middle_ref[...] = middle
    mid_hat, _ = normed(middle, mask, width)
    two = ((mid_hat * fg[...] + fb[...]) * mask).astype(BF16)
    pooled_ref[...] = middle + bn[...]
    hidden_width = jnp.where(is_text, MLP_TXT, full_hidden)
    hidden_mask = (iota((1, full_hidden), 1) < hidden_width).astype(F32)

    def forward(at):
        pre = mm(two, s_ww[:, at]) + bw[:, at]
        gate = sigmoid(1.702 * pre)
        active = pre * gate * hidden_mask[:, at]
        slope_ref[:, at] = (gate + 1.702 * active * (1.0 - gate)) * hidden_mask[:, at]
        pooled_ref[...] += mm(active.astype(BF16), s_wn[at, :])

    hidden.each(forward)
    out_hat, out_inv = normed(pooled_ref[...], mask, width)
    early_ref[:, 2 * full_width : 3 * full_width] = out_hat.astype(BF16)
    lane = iota((pairs, 128), 1)
    numbers = jnp.zeros((pairs, 128), F32)
    for place in range(3):
        part = out_inv.astype(BF16).astype(F32)
        numbers = jnp.where(lane == place, part, numbers)
        out_inv = out_inv - part
    early_ref[:, 3 * full_width :] = numbers.astype(BF16)
    three = ((out_hat * lg[...] + lb[...]) * mask).astype(BF16)
    get_we.wait()
    embedded = mm(three, s_we[...])
    embedded_ref[...] = embedded
    unit_ref[...] = (
        embedded * lax.rsqrt(jnp.sum(embedded * embedded, axis=-1, keepdims=True) + 1e-06)
    ).astype(BF16)
    keys_ref[...] = mm_nt(wide, s_triple[1]).astype(BF16)
    hat_rows_ref[...] = mm(pick, s_hat[...]).astype(BF16)
    for copy in (put_hat, put_inv, put_probs):
        copy.wait()


def means_kernel(dims, ag, ab, hat_ref, probs_ref, turned_ref, spread_ref, s_turn):
    pairs, tokens, full_width, full_hidden = dims
    _, width, mask = tower_sizes(full_width, full_hidden)
    rows = probs_ref.shape[0]
    low = probs_ref[...].astype(BF16)
    spread = mm(low, hat_ref[...])
    spread_ref[...] = spread
    total = jnp.sum(low.astype(F32), axis=1, keepdims=True)
    s_turn[rows:, :] = jnp.zeros((s_turn.shape[0] - rows, full_width), F32)
    s_turn[0:rows, :] = (spread * ag[...] + total * ab[...]) * mask
    turned_ref[...] = s_turn[...].T.astype(BF16)


def in_order(pieces, stages, pairs, block, at):
    here = lax.axis_index("dp")
    row = at + iota((block, 1), 0)
    owner = lax.div(row, pairs)
    apart = lax.bitwise_xor(owner, here)
    place = jnp.zeros_like(owner)
    weight = 1
    for shift, bits in stages:
        digit = lax.bitwise_and(lax.shift_right_logical(apart, shift), (1 << bits) - 1)
        place = place + digit * weight
        weight = weight << bits
    column = place * pairs + row - owner * pairs
    total = None
    first = 0
    for piece in pieces:
        count = piece.shape[0]
        part = mm(one_hot(iota((block, count), 1) + first == column), piece[...])
        total = part if total is None else total + part
        first += count
    return total.astype(BF16)


def over_blocks(count, step):
    if count == 1:
        step(0)
    else:

        def one(index, carry):
            step(index)
            return carry

        lax.fori_loop(0, count, one, 0)


def block_rows(total):
    return 320 if total % 320 == 0 else total


def loss_kernel(
    dims,
    own_rel,
    other_rel,
    flags_ref,
    logit_scale,
    loss_scale,
    ag,
    ab,
    triple_hbm,
    triple_bias,
    wo_hbm,
    fg,
    ww_hbm,
    wn_hbm,
    lg,
    we_hbm,
    hat_hbm,
    probs_hbm,
    spread_ref,
    keys_ref,
    embedded_ref,
    pooled_ref,
    middle_ref,
    slope_ref,
    hat_rows_ref,
    turned_ref,
    loss_ref,
    hits_ref,
    scale_ref,
    grad_all_ref,
    late_ref,
    rows_ref,
    back_ref,
    values_ref,
    rows_one_ref,
    rows_mid_ref,
    s_own,
    s_other,
    s_triple,
    s_wo,
    s_ww,
    s_wn,
    s_we,
    s_hat,
    s_probs,
    s_rows,
    s_two,
    s_turn,
    sems,
    hidden_sems,
):
    pairs, tokens, full_width, full_hidden, stages = dims
    all_pairs = own_rel.shape[0]
    block = block_rows(all_pairs)
    here = lax.axis_index("dp")
    is_text, width, mask = tower_sizes(full_width, full_hidden)
    rows = full_width // HEAD * pairs
    get_we = fetch(we_hbm.at[0], s_we, sems.at[0])
    hidden = Hidden(ww_hbm, wn_hbm, s_ww, s_wn, hidden_sems, full_hidden // CHUNK)
    hidden.start((1, 0))
    get_wo = fetch(wo_hbm.at[0], s_wo, sems.at[1])
    get_triple = fetch(triple_hbm.at[0], s_triple, sems.at[2])
    get_hat = fetch(hat_hbm, s_hat, sems.at[3])
    get_probs = fetch(probs_hbm, s_probs, sems.at[4])

    def place(index):
        at = pl.multiple_of(index * block, block)
        s_own[pl.ds(at, block), :] = in_order([own_rel], stages, pairs, block, at)
        s_other[pl.ds(at, block), :] = in_order([other_rel], stages, pairs, block, at)

    over_blocks(all_pairs // block, place)
    live = (flags_ref[...] > 0).astype(F32)
    live_pairs = jnp.sum(live, axis=1, keepdims=True)
    factor = jnp.exp(logit_scale[...])
    row_weight = loss_scale[...] / (2.0 * live_pairs)
    loss_ref[...] = jnp.zeros_like(loss_ref)
    hits_ref[...] = jnp.zeros_like(hits_ref)
    scale_ref[...] = jnp.zeros_like(scale_ref)
    grad_all_ref[...] = jnp.zeros_like(grad_all_ref)

    def part(index):
        at = pl.multiple_of(index * block, block)
        eye = at + iota((block, all_pairs), 0) == iota((block, all_pairs), 1)
        live_rows = jnp.sum(jnp.where(eye, live, 0.0), axis=1, keepdims=True)

        def one_way(left, right):
            logits = mm_nt(left, right) * factor
            masked = jnp.where(live > 0.5, logits, -1e30)
            peak = jnp.max(masked, axis=1, keepdims=True)
            powers = jnp.exp(masked - peak)
            total = jnp.sum(powers, axis=1, keepdims=True)
            log_total = peak + jnp.log(total)
            matched = jnp.sum(jnp.where(eye, logits, 0.0), axis=1, keepdims=True)
            gap = jnp.where(live_rows > 0.5, log_total - matched, 0.0)
            grads = (
                (powers / total - eye.astype(F32)) * (live_rows * row_weight)
            ).astype(BF16)
            loss = jnp.sum(live_rows * gap, axis=0, keepdims=True)
            hits = jnp.sum(live_rows * jnp.exp(-gap), axis=0, keepdims=True)
            scale = jnp.sum(
                jnp.sum(grads.astype(F32) * logits, axis=1, keepdims=True),
                axis=0,
                keepdims=True,
            )
            return grads, loss, hits, scale

        own = s_own[pl.ds(at, block), :]
        other = s_other[pl.ds(at, block), :]
        grads, loss_one, hits_one, scale_one = one_way(own, s_other[...])
        grad_all_ref[pl.ds(at, block), :] += factor * mm(grads, s_other[...])
        grads, loss_two, hits_two, scale_two = one_way(other, s_own[...])
        grad_all_ref[...] += factor * mm_tn(grads, other)
        loss_ref[...] += loss_one + loss_two
        hits_ref[...] += hits_one + hits_two
        scale_ref[...] += scale_one + scale_two

    over_blocks(all_pairs // block, part)
    loss_ref[...] = loss_ref[...] / (2.0 * live_pairs)
    hits_ref[...] = hits_ref[...] / (2.0 * live_pairs)

    for pair in range(pairs):
        s_rows[pair : pair + 1, :] = grad_all_ref[pl.ds(here * pairs + pair, 1), :]

    gain, shift = ag[...] * mask, ab[...] * mask
    grad_embed = embed_back(embedded_ref[...], s_rows[...])
    get_we.wait()
    grad_three = mm_nt(grad_embed, s_we[...])
    out_hat, out_inv = normed(pooled_ref[...], mask, width)
    grad_pooled = norm_back(out_hat, out_inv, lg[...] * mask, grad_three, mask, width)
    branch = grad_pooled.astype(BF16)
    s_two[...] = jnp.zeros_like(s_two)

    def backward(at):
        grad_active = mm_nt(branch, s_wn[at, :])
        grad_hidden = (grad_active * slope_ref[:, at]).astype(BF16)
        s_two[...] += mm_nt(grad_hidden, s_ww[:, at])

    hidden.each(backward)
    mid_hat, mid_inv = normed(middle_ref[...], mask, width)
    grad_two = s_two[...] * mask
    grad_middle = grad_pooled + norm_back(mid_hat, mid_inv, fg[...] * mask, grad_two, mask, width)
    rows_mid_ref[...] = grad_middle
    attention = grad_middle.astype(BF16)
    rows_ref[:, full_width:] = attention
    get_wo.wait()
    grad_mixed = (mm_nt(attention, s_wo[...]) * mask).astype(BF16)
    repeat = repeat_rows(rows, pairs)
    heads = head_mask(rows, pairs, full_width)
    wide = jnp.where(heads, mm(repeat, grad_mixed), 0.0)
    get_triple.wait()
    along = mm_nt(wide.astype(BF16), s_triple[2])
    values_low = along.astype(BF16)
    values_ref[...] = values_low
    offset = jnp.sum(along * shift, axis=1, keepdims=True) + jnp.sum(
        wide * triple_bias[0, 1:2, :], axis=1, keepdims=True
    )
    get_hat.wait()
    get_probs.wait()
    grad_probs = mm_nt((along * gain).astype(BF16), s_hat[...]) + offset
    probs = s_probs[...]
    inner = jnp.sum(grad_probs * probs, axis=1, keepdims=True)
    back = (probs * (grad_probs - inner)).astype(BF16)
    back_ref[...] = back
    spread = mm(back, s_hat[...])
    total = jnp.sum(back.astype(F32), axis=1, keepdims=True)
    means = (spread * gain + total * shift).astype(BF16)
    query_wide = mm(means, s_triple[1]) * 0.125
    grad_query = mm_tn(repeat, jnp.where(heads, query_wide, 0.0).astype(BF16)).astype(BF16)
    rows_ref[:, 0:full_width] = grad_query
    rows_one = mm_nt(grad_query, s_triple[0]) * mask
    rows_one_ref[...] = rows_one
    values_wide = values_low.astype(F32)
    keys_wide = keys_ref[...].astype(F32)
    prob_total = jnp.sum(probs.astype(BF16).astype(F32), axis=1, keepdims=True)
    gain_sum = (
        sums_of(values_wide * spread_ref[...])
        + sums_of(keys_wide * spread)
        + sums_of(rows_one * hat_rows_ref[...].astype(F32))
    )
    shift_sum = (
        sums_of(values_wide * prob_total) + sums_of(keys_wide * total) + sums_of(rows_one)
    ) * mask
    s_turn[rows:, :] = jnp.zeros((s_turn.shape[0] - rows, full_width), F32)
    s_turn[0:rows, :] = means.astype(F32)
    slot = rows
    for vector in (gain_sum, shift_sum, sums_of(grad_two * mid_hat), sums_of(grad_two)):
        for _ in range(3):
            low = vector.astype(BF16).astype(F32)
            s_turn[slot : slot + 1, :] = low
            vector = vector - low
            slot += 1
    late_ref[:, 0 : s_turn.shape[0]] = s_turn[...].T.astype(BF16)
    late_ref[:, s_turn.shape[0] :] = turned_ref[...]


def stream_kernel(
    dims,
    ends_ref,
    ag,
    hat_hbm,
    inv_hbm,
    probs_hbm,
    back_ref,
    values_ref,
    keys_ref,
    rows_one_ref,
    rows_mid_ref,
    out_hbm,
    s_hat,
    s_inv,
    s_probs,
    s_left,
    s_right,
    s_out,
    sems,
    out_sems,
):
    pairs, tokens, full_width, full_hidden = dims
    is_text, width, mask = tower_sizes(full_width, full_hidden)
    rows = full_width // HEAD * pairs
    get_probs = fetch(probs_hbm, s_probs, sems.at[0])
    get_hat = fetch(hat_hbm, s_hat, sems.at[1])
    get_inv = fetch(inv_hbm, s_inv, sems.at[2])
    gain = ag[...] * mask
    s_left[rows : 2 * rows, :] = back_ref[...]
    s_right[0:rows, :] = values_ref[...]
    s_right[rows : 2 * rows, :] = keys_ref[...]
    spots = pooled_spots(ends_ref, is_text, pairs, 3)
    s_left[2 * rows :, :] = one_hot(iota((3 * pairs, tokens), 1).astype(F32) == spots)
    s_right[2 * rows :, :] = three_parts(rows_one_ref[...])
    middle_parts = three_parts(rows_mid_ref[...])
    ones = one_hot(iota((full_width, 128), 0).astype(F32) < width)
    get_probs.wait()
    s_left[0:rows, :] = s_probs[...].astype(BF16)
    get_hat.wait()
    get_inv.wait()

    def put(at, count):
        spot = pl.ds(at, count)
        return pltpu.make_async_copy(
            s_out.at[spot, :], out_hbm.at[0, spot, :], out_sems.at[at // NORM_ROWS]
        )

    def norm_rows(at, count):
        spot = pl.ds(at, count)
        upward = mm_tn(s_left[:, spot], s_right[...])
        hat = s_hat[spot, :].astype(F32)
        scaled = upward * gain
        mean = mm(scaled.astype(BF16), ones) / width
        along = mm((scaled * hat).astype(BF16), ones) / width
        s_out[spot, :] = across(s_inv[spot, :], full_width) * (
            scaled - across(mean, full_width) * mask - hat * across(along, full_width)
        ) + mm_tn(s_left[2 * rows :, spot], middle_parts)
        put(at, count).start()

    over_tokens(tokens, NORM_ROWS, norm_rows)
    over_tokens(tokens, NORM_ROWS, lambda at, count: put(at, count).wait())


def window_of(slice_hidden, full_hidden):
    here = lax.axis_index("dp")
    first = jnp.minimum(lax.div(here * slice_hidden, 128) * 128, full_hidden - WINDOW)
    return pl.multiple_of(first, 128)


def rows_kernel(dims, *refs):
    pairs, full_width, full_hidden, slice_width, slice_hidden, stages, pieces = dims
    early = refs[:pieces]
    (
        grad_ref,
        ag,
        ab,
        triple_hbm,
        triple_bias,
        wo_hbm,
        bo,
        fg,
        fb,
        ww_hbm,
        bw_hbm,
        wn_hbm,
        lg,
        lb,
        we_hbm,
        ones_ref,
        queries_ref,
        mixed_ref,
        embed_ref,
        narrow_ref,
        widen_ref,
        final_gain_ref,
        final_bias_ref,
        narrow_bias_ref,
        widen_bias_ref,
        s_triple,
        s_wo,
        s_ww,
        s_wn,
        s_we,
        s_bw,
        s_vectors,
        sems,
    ) = refs[pieces:]
    all_pairs = grad_ref.shape[0]
    block = block_rows(all_pairs)
    here = lax.axis_index("dp")
    is_text, width, mask = tower_sizes(full_width, full_hidden)
    first = window_of(slice_hidden, full_hidden)
    window = pl.ds(first, WINDOW)
    copies = [
        fetch(triple_hbm.at[0, 0], s_triple, sems.at[0]),
        fetch(wo_hbm.at[0], s_wo, sems.at[1]),
        fetch(we_hbm.at[0], s_we, sems.at[2]),
        fetch(ww_hbm.at[0, :, window], s_ww, sems.at[3]),
        fetch(wn_hbm.at[0, window, :], s_wn, sems.at[4]),
        fetch(bw_hbm.at[:, window], s_bw, sems.at[5]),
    ]
    for ref in (embed_ref, narrow_ref, widen_ref, widen_bias_ref, s_vectors):
        ref[...] = jnp.zeros_like(ref)
    lane = iota((full_width, slice_width), 0)
    pick = one_hot(
        (lane == here * slice_width + iota((full_width, slice_width), 1))
        & (lane.astype(F32) < width)
    )
    unit = first + iota((WINDOW, slice_hidden), 0)
    hidden = jnp.where(is_text, MLP_TXT, full_hidden)
    chosen = one_hot(
        (unit == here * slice_hidden + iota((WINDOW, slice_hidden), 1)) & (unit < hidden)
    )
    gain, shift = lg[...] * mask, lb[...] * mask
    for copy in copies:
        copy.wait()

    def part(index):
        at = pl.multiple_of(index * block, block)
        here_rows = pl.ds(at, block)
        arrived = in_order(early, stages, pairs, block, at)
        mixed = arrived[:, 0:full_width]
        stream_rows = arrived[:, full_width : 2 * full_width].astype(F32)
        out_hat = arrived[:, 2 * full_width : 3 * full_width].astype(F32)
        out_inv = jnp.sum(arrived[:, 3 * full_width :].astype(F32), axis=1, keepdims=True)
        rows_hat, _ = normed(stream_rows, mask, width)
        one = ((rows_hat * ag[...] + ab[...]) * mask).astype(BF16)
        ones_ref[here_rows, :] = mm(one, pick).astype(BF16)
        query = (mm(one, s_triple[...]) + triple_bias[0, 0:1, :]) * mask
        queries_ref[here_rows, :] = query.astype(BF16)
        mixed_ref[here_rows, :] = mm(mixed, pick).astype(BF16)
        middle = stream_rows + mm(mixed, s_wo[...]) + bo[...]
        mid_hat, _ = normed(middle, mask, width)
        two = ((mid_hat * fg[...] + fb[...]) * mask).astype(BF16)
        pre = mm(two, s_ww[...]) + s_bw[...]
        gate = sigmoid(1.702 * pre)
        active = pre * gate
        slope = gate + 1.702 * active * (1.0 - gate)
        three = (out_hat * gain + shift).astype(BF16)
        grad_embed = embed_back(mm(three, s_we[...]), grad_ref[here_rows, :])
        embed_ref[0] += mm_tn(mm(three, pick).astype(BF16), grad_embed)
        grad_three = mm_nt(grad_embed, s_we[...])
        s_vectors[0:1, :] += sums_of(grad_three * out_hat)
        s_vectors[1:2, :] += sums_of(grad_three)
        branch = norm_back(out_hat, out_inv, gain, grad_three, mask, width).astype(BF16)
        s_vectors[2:3, :] += sums_of(branch.astype(F32))
        narrow_ref[0] += mm_tn(mm(active.astype(BF16), chosen).astype(BF16), branch)
        grad_hidden = (mm_nt(branch, s_wn[...]) * slope).astype(BF16)
        hidden_slice = mm(grad_hidden, chosen)
        widen_ref[0] += mm_tn(hidden_slice.astype(BF16), two)
        widen_bias_ref[...] += sums_of(hidden_slice)

    over_blocks(all_pairs // block, part)
    vectors = dot_dims(s_vectors[...], pick.astype(F32), 1, 0, lax.Precision.HIGHEST)
    for slot, ref in enumerate((final_gain_ref, final_bias_ref, narrow_bias_ref)):
        ref[...] = vectors[slot : slot + 1, :]


def last_kernel(dims, *refs):
    pairs, full_width, full_hidden, slice_width, stages, pieces = dims
    arrived = refs[:pieces]
    (
        late_ref,
        ones_ref,
        queries_ref,
        mixed_ref,
        wo_hbm,
        triple_ref,
        mixer_ref,
        gain_ref,
        shift_ref,
        feed_gain_ref,
        feed_bias_ref,
        mixer_bias_ref,
        bias_ref,
        s_keys,
        s_means,
        s_late,
        s_values,
        s_sums,
        s_wo,
        sems,
    ) = refs[pieces:]
    here = lax.axis_index("dp")
    is_text, width, mask = tower_sizes(full_width, full_hidden)
    get_wo = fetch(wo_hbm.at[0], s_wo, sems.at[0])
    count = late_ref.shape[0]
    lanes = late_ref.shape[2] // 2
    heads = full_width // HEAD
    rows = heads * pairs
    all_pairs = queries_ref.shape[0]
    block = block_rows(all_pairs)
    triple_ref[0, 0] = jnp.zeros((slice_width, full_width), F32)
    mixer_ref[...] = jnp.zeros_like(mixer_ref)
    s_late[...] = jnp.zeros_like(s_late)
    s_sums[...] = jnp.zeros_like(s_sums)
    get_wo.wait()

    def part(index):
        at = pl.multiple_of(index * block, block)
        here_rows = pl.ds(at, block)
        now = in_order(arrived, stages, pairs, block, at)
        grad_query = now[:, 0:full_width]
        attention = now[:, full_width:]
        triple_ref[0, 0] += mm_tn(ones_ref[here_rows, :], grad_query)
        mixer_ref[0] += mm_tn(mixed_ref[here_rows, :], attention)
        grad_mixed = (mm_nt(attention, s_wo[...]) * mask).astype(BF16)
        s_values[here_rows, :] = grad_mixed
        for slot, vector in enumerate((grad_query, grad_mixed, attention)):
            s_sums[slot : slot + 1, :] += sums_of(vector.astype(F32))

    over_blocks(all_pairs // block, part)
    if slice_width % 16 == 0 and count <= 16:
        for source in range(count):
            now = late_ref[source]
            s_late[...] += now[:, 0:lanes].astype(F32)
            across_now = slice(source * pairs, (source + 1) * pairs)
            for head in range(heads):
                down = slice(head * slice_width, (head + 1) * slice_width)
                lane = head * pairs
                s_keys[down, across_now] = now[:, lane : lane + pairs]
                s_means[down, across_now] = now[:, lanes + lane : lanes + lane + pairs]
        left = iota((slice_width, 2 * HEAD), 1) < HEAD
        for two in range(heads // 2):
            down = slice(two * 2 * slice_width, (two + 1) * 2 * slice_width)
            lane = slice(two * 2 * HEAD, (two + 1) * 2 * HEAD)
            both = mm(s_keys[down, :], queries_ref[:, lane]) * 0.125
            triple_ref[0, 1, :, lane] = jnp.where(left, both[0:slice_width], both[slice_width:])
            both = mm(s_means[down, :], s_values[:, lane])
            triple_ref[0, 2, :, lane] = jnp.where(left, both[0:slice_width], both[slice_width:])
    else:
        triple_ref[0, 1] = jnp.zeros((slice_width, full_width), F32)
        triple_ref[0, 2] = jnp.zeros((slice_width, full_width), F32)
        head = head_mask(lanes, pairs, full_width)

        def one(source, carry):
            now = late_ref[source]
            s_late[...] += now[:, 0:lanes].astype(F32)
            row = iota((lanes, all_pairs), 0)
            column = iota((lanes, all_pairs), 1)
            repeat = one_hot((column == source * pairs + lax.rem(row, pairs)) & (row < rows))
            for which, origin in ((1, queries_ref), (2, s_values)):
                wide = jnp.where(head, mm(repeat, origin[...]), 0.0).astype(BF16)
                first = (which - 1) * lanes
                triple_ref[0, which] += mm(now[:, first : first + lanes], wide)
            return carry

        lax.fori_loop(0, count, one, 0)
        triple_ref[0, 1] = triple_ref[0, 1] * 0.125
    lane = iota((8, lanes), 1)
    row = iota((8, lanes), 0)
    slot = rows + row * 3
    chosen = ((lane >= slot) & (lane < slot + 3) & (row < 4)).astype(F32)
    from_late = dot_dims(chosen, s_late[...], 1, 1, lax.Precision.HIGHEST)
    for slot, ref in enumerate((gain_ref, shift_ref, feed_gain_ref, feed_bias_ref)):
        ref[...] = from_late[slot : slot + 1, :]
    pick = (
        iota((full_width, slice_width), 0)
        == here * slice_width + iota((full_width, slice_width), 1)
    ).astype(F32)
    sums = dot_dims(s_sums[...], pick, 1, 0, lax.Precision.HIGHEST)
    bias_ref[0] = sums[0:2, :]
    mixer_bias_ref[...] = sums[2:3, :]


def stages_of(count):
    bits = count.bit_length() - 1
    stages = []
    while bits > 0:
        take = 2 if bits >= 2 else 1
        bits -= take
        stages.append((bits, take))
    return tuple(stages)


def exchange(block, axis, stage):
    count = lax.axis_size(axis)
    shift, bits = stage
    parts = [block]
    for apart in range(1, 1 << bits):
        route = [(low, low ^ (apart << shift)) for low in range(count)]
        parts.append(lax.ppermute(block, axis, route))
    return parts


def call(kernel, ins, outs, scratch, in_hbm=(), out_hbm=(), cost=None):
    vmem = pl.BlockSpec(memory_space=pltpu.VMEM)
    anywhere = pl.BlockSpec(memory_space=pl.ANY)
    specs = [anywhere if index in in_hbm else vmem for index in range(len(ins))]
    out_specs = [anywhere if index in out_hbm else vmem for index in range(len(outs))]
    flops, moved = cost
    return pl.pallas_call(
        kernel,
        out_shape=[jax.ShapeDtypeStruct(shape, kind) for shape, kind in outs],
        in_specs=specs,
        out_specs=out_specs,
        scratch_shapes=scratch,
        compiler_params=pltpu.CompilerParams(vmem_limit_bytes=VMEM_LIMIT),
        cost_estimate=pl.CostEstimate(flops=flops, bytes_accessed=moved, transcendentals=0),
    )(*ins)


def body(
    block_input,
    segments,
    caption_ends,
    pair_flags,
    attention_gain,
    attention_bias,
    triple_weight,
    triple_bias,
    mixer_weight,
    mixer_bias,
    feed_gain,
    feed_bias,
    widen_weight,
    widen_bias,
    narrow_weight,
    narrow_bias,
    final_gain,
    final_bias,
    embed_weight,
    logit_scale,
    loss_scale,
):
    tokens, width = block_input.shape[1:]
    hidden = widen_weight.shape[2]
    emb = embed_weight.shape[2]
    pairs = caption_ends.shape[0]
    count = lax.axis_size("dp")
    all_pairs = pair_flags.shape[0]
    heads = width // HEAD
    rows = heads * pairs
    lanes = -(-(rows + 12) // 128) * 128
    slice_width = width // count
    slice_hidden = hidden // count
    stages = stages_of(count)
    ends = caption_ends.reshape(1, pairs)
    dma = pltpu.SemaphoreType.DMA
    weights_scratch = [
        pltpu.VMEM((3, width, width), BF16),
        pltpu.VMEM((width, width), BF16),
        pltpu.VMEM((width, hidden), BF16),
        pltpu.VMEM((hidden, width), BF16),
        pltpu.VMEM((width, emb), BF16),
    ]
    dims = (pairs, tokens, width, hidden)
    chunk_count = hidden // CHUNK
    (
        unit,
        early,
        hat,
        invert,
        probs,
        keys,
        embedded,
        pooled,
        middle,
        slope,
        hat_rows,
    ) = call(
        partial(attend_kernel, dims),
        (
            ends,
            block_input,
            attention_gain,
            attention_bias,
            triple_weight,
            triple_bias,
            mixer_weight,
            mixer_bias,
            feed_gain,
            feed_bias,
            widen_weight,
            widen_bias,
            narrow_weight,
            narrow_bias,
            final_gain,
            final_bias,
            embed_weight,
        ),
        [
            ((pairs, emb), BF16),
            ((pairs, 3 * width + 128), BF16),
            ((tokens, width), BF16),
            ((tokens, 128), F32),
            ((rows, tokens), F32),
            ((rows, width), BF16),
            ((pairs, emb), F32),
            ((pairs, width), F32),
            ((pairs, width), F32),
            ((pairs, hidden), F32),
            ((pairs, width), BF16),
        ],
        [
            pltpu.VMEM((tokens, width), BF16),
            pltpu.VMEM((tokens, width), BF16),
            pltpu.VMEM((tokens, width), BF16),
            pltpu.VMEM((tokens, 128), F32),
            pltpu.VMEM((rows, tokens), F32),
            pltpu.VMEM((tokens, width), BF16),
            pltpu.VMEM((tokens, width), BF16),
        ]
        + weights_scratch
        + [
            pltpu.VMEM((rows, tokens), BF16),
            dma((7,)),
            dma((2, chunk_count)),
        ],
        in_hbm=(1, 4, 6, 10, 12, 16),
        out_hbm=(2, 3, 4),
        cost=(10**9, 20 * 10**6),
    )
    turned, spread = call(
        partial(means_kernel, dims),
        (attention_gain, attention_bias, hat, probs),
        [((width, lanes), BF16), ((rows, width), F32)],
        [pltpu.VMEM((lanes, width), F32)],
        cost=(10**9, 5 * 10**6),
    )
    early_pieces = [early]
    own_rel = unit
    for index, stage in enumerate(stages):
        own_parts = exchange(own_rel, "dp", stage)
        if index + 1 < len(stages):
            early_parts = exchange(jnp.concatenate(early_pieces, axis=0), "dp", stage)
            own_parts, early_pieces, turned, spread = lax.optimization_barrier(
                (own_parts, early_parts, turned, spread)
            )
        own_rel = jnp.concatenate(own_parts, axis=0)
    other_rel = lax.ppermute(own_rel, "tower", [(0, 1), (1, 0)])
    early_pieces = exchange(jnp.concatenate(early_pieces, axis=0), "dp", stages[-1])
    (
        loss,
        hits,
        scale,
        grad_all,
        late,
        late_rows,
        back,
        values,
        rows_one,
        rows_mid,
    ) = call(
        partial(loss_kernel, dims + (stages,)),
        (
            own_rel,
            other_rel,
            pair_flags.reshape(1, all_pairs),
            logit_scale.reshape(1, 1),
            loss_scale.reshape(1, 1),
            attention_gain,
            attention_bias,
            triple_weight,
            triple_bias,
            mixer_weight,
            feed_gain,
            widen_weight,
            narrow_weight,
            final_gain,
            embed_weight,
            hat,
            probs,
            spread,
            keys,
            embedded,
            pooled,
            middle,
            slope,
            hat_rows,
            turned,
        ),
        [
            ((1, 1), F32),
            ((1, 1), F32),
            ((1, 1), F32),
            ((all_pairs, emb), F32),
            ((width, 2 * lanes), BF16),
            ((pairs, 2 * width), BF16),
            ((rows, tokens), BF16),
            ((rows, width), BF16),
            ((pairs, width), F32),
            ((pairs, width), F32),
        ],
        [pltpu.VMEM((all_pairs, emb), BF16), pltpu.VMEM((all_pairs, emb), BF16)]
        + weights_scratch
        + [
            pltpu.VMEM((tokens, width), BF16),
            pltpu.VMEM((rows, tokens), F32),
            pltpu.VMEM((pairs, emb), F32),
            pltpu.VMEM((pairs, width), F32),
            pltpu.VMEM((lanes, width), F32),
            dma((5,)),
            dma((2, chunk_count)),
        ],
        in_hbm=(7, 9, 11, 12, 14, 15, 16),
        cost=(10**9, 20 * 10**6),
    )
    early_pieces, late, late_rows = lax.optimization_barrier((early_pieces, late, late_rows))
    late_all = lax.all_to_all(late, "dp", 0, 0, tiled=True).reshape(
        count, slice_width, 2 * lanes
    )
    late_pieces = [late_rows]
    for stage in stages:
        late_pieces = exchange(jnp.concatenate(late_pieces, axis=0), "dp", stage)
    (block_grad,) = call(
        partial(stream_kernel, dims),
        (ends, attention_gain, hat, invert, probs, back, values, keys, rows_one, rows_mid),
        [((1, tokens, width), F32)],
        [
            pltpu.VMEM((tokens, width), BF16),
            pltpu.VMEM((tokens, 128), F32),
            pltpu.VMEM((rows, tokens), F32),
            pltpu.VMEM((2 * rows + 3 * pairs, tokens), BF16),
            pltpu.VMEM((2 * rows + 3 * pairs, width), BF16),
            pltpu.VMEM((tokens, width), F32),
            dma((3,)),
            dma((-(-tokens // NORM_ROWS),)),
        ],
        in_hbm=(2, 3, 4),
        out_hbm=(0,),
        cost=(2 * 10**9, 10 * 10**6),
    )
    ahead = len(early_pieces)
    vector = ((1, slice_width), F32)
    (
        ones,
        query_rows,
        mixed_slice,
        grad_embed,
        grad_narrow,
        grad_widen,
        grad_final_gain,
        grad_final_bias,
        grad_narrow_bias,
        grad_widen_bias,
    ) = call(
        partial(rows_kernel, (pairs, width, hidden, slice_width, slice_hidden, stages, ahead)),
        tuple(early_pieces)
        + (
            grad_all,
            attention_gain,
            attention_bias,
            triple_weight,
            triple_bias,
            mixer_weight,
            mixer_bias,
            feed_gain,
            feed_bias,
            widen_weight,
            widen_bias,
            narrow_weight,
            final_gain,
            final_bias,
            embed_weight,
        ),
        [
            ((all_pairs, slice_width), BF16),
            ((all_pairs, width), BF16),
            ((all_pairs, slice_width), BF16),
            ((1, slice_width, emb), F32),
            ((1, slice_hidden, width), F32),
            ((1, slice_hidden, width), F32),
            vector,
            vector,
            vector,
            ((1, slice_hidden), F32),
        ],
        [
            pltpu.VMEM((width, width), BF16),
            pltpu.VMEM((width, width), BF16),
            pltpu.VMEM((width, WINDOW), BF16),
            pltpu.VMEM((WINDOW, width), BF16),
            pltpu.VMEM((width, emb), BF16),
            pltpu.VMEM((1, WINDOW), F32),
            pltpu.VMEM((8, width), F32),
            dma((6,)),
        ],
        in_hbm=tuple(ahead + index for index in (3, 5, 9, 10, 11, 14)),
        cost=(3 * 10**9, 10 * 10**6),
    )
    (
        grad_triple,
        grad_mixer,
        grad_gain,
        grad_bias,
        grad_feed_gain,
        grad_feed_bias,
        grad_mixer_bias,
        grad_triple_bias,
    ) = call(
        partial(last_kernel, (pairs, width, hidden, slice_width, stages, len(late_pieces))),
        tuple(late_pieces) + (late_all, ones, query_rows, mixed_slice, mixer_weight),
        [
            ((1, 3, slice_width, width), F32),
            ((1, slice_width, width), F32),
            vector,
            vector,
            vector,
            vector,
            vector,
            ((1, 2, slice_width), F32),
        ],
        [
            pltpu.VMEM((width // HEAD * slice_width, all_pairs), BF16),
            pltpu.VMEM((width // HEAD * slice_width, all_pairs), BF16),
            pltpu.VMEM((slice_width, lanes), F32),
            pltpu.VMEM((all_pairs, width), BF16),
            pltpu.VMEM((8, width), F32),
            pltpu.VMEM((width, width), BF16),
            dma((1,)),
        ],
        in_hbm=(len(late_pieces) + 4,),
        cost=(10**9, 10 * 10**6),
    )
    return (
        loss[0, 0],
        hits[0, 0],
        block_grad,
        grad_gain,
        grad_bias,
        grad_triple,
        grad_triple_bias,
        grad_mixer,
        grad_mixer_bias,
        grad_feed_gain,
        grad_feed_bias,
        jnp.swapaxes(grad_widen, 1, 2),
        grad_widen_bias,
        grad_narrow,
        grad_narrow_bias,
        grad_final_gain,
        grad_final_bias,
        grad_embed,
        scale[0, 0],
    )


def solution(mesh):
    in_specs = (
        P("tower", "dp", None),
        P("dp", None),
        P("dp"),
        P(),
        P("tower", None),
        P("tower", None),
        P("tower", None, None, None),
        P("tower", None, None),
        P("tower", None, None),
        P("tower", None),
        P("tower", None),
        P("tower", None),
        P("tower", None, None),
        P("tower", None),
        P("tower", None, None),
        P("tower", None),
        P("tower", None),
        P("tower", None),
        P("tower", None, None),
        P(),
        P(),
    )
    out_specs = (
        P(),
        P(),
        P("tower", "dp", None),
        P("tower", "dp"),
        P("tower", "dp"),
        P("tower", None, "dp", None),
        P("tower", None, "dp"),
        P("tower", "dp", None),
        P("tower", "dp"),
        P("tower", "dp"),
        P("tower", "dp"),
        P("tower", None, "dp"),
        P("tower", "dp"),
        P("tower", "dp", None),
        P("tower", "dp"),
        P("tower", "dp"),
        P("tower", "dp"),
        P("tower", "dp", None),
        P(),
    )
    return jax.shard_map(body, mesh=mesh, in_specs=in_specs, out_specs=out_specs, check_vma=False)
```

time: 2370 us -> 116 us (0.05)
  waiting for transfers between devices: 1790 us -> 22.5 us
  local copies, waits for them, and re-layouts: 189 us -> 2.76 us
  matrix products: 147 us -> 0 us
  blocking collectives: 130 us -> 0 us
  Pallas kernels: 0 us -> 57.8 us
  other arithmetic: 53.5 us -> 0.19 us
  loops' own time: 26.3 us -> 0 us
    unnamed x28 -> x0, waiting for transfers between devices: 1020 us -> none
    reduce_scatter x5 -> x0, waiting for transfers between devices: 769 us -> none  [the longest x1 176 us: body(): lax.psum_scatter(upper_grads[4], 'dp', scatter_dimension=1, tiled=True)]
    dot_general x31 -> x0, matrix products: 147 us -> none  [the longest x8 42.1 us: dot_second(): lax.dot_general(left, right, (((1,), (1,)), ((), ())), preferred_element_...]
    pallas_call x0 -> x6, Pallas kernels: none -> 57.8 us  [call(): pl.pallas_call(kernel, out_shape=[jax.ShapeDtypeStruct(shape, kind) for s...]
    all_gather x1 -> x0, blocking collectives: 47 us -> none  [body(): others = lax.all_gather(partner, 'dp', axis=0, tiled=True)]
    convert_element_type x12 -> x0, local copies, waits for them, and re-layouts: 44.5 us -> none  [the longest x2 10.7 us: tower_back_lower(): grad_keys = (jnp.einsum('ghqk,gqhd->gkhd', grad_scores, query.reshape(sha...]
    unnamed x1 -> x0, blocking collectives: 43 us -> none
    psum x1 -> x0, blocking collectives: 40 us -> none  [body(): totals = lax.psum((loss_part, hits_part, scale_part), ('tower', 'dp'))]
  transfers between devices with their start and end apart: 20 -> 20, of which waited for: 15 -> 6; matrix products, arithmetic and copies ran while one was open for 8% -> 1% of each run, Pallas kernels for 0% -> 32%
where the time goes in v1:
time: 116 us; the launch traced here: 115 us
  Pallas kernels  57.8 us (50%)
  starting transfers between devices  29.8 us (26%)
  waiting for transfers between devices  22.5 us (19%)
  local copies, waits for them, and re-layouts  2.76 us (2%)
  between operations  2.46 us (2%)
    pallas_call x6, Pallas kernels, call(): pl.pallas_call(kernel, out_shape=[jax.ShapeDtypeStruct(shape, kind) for s...  57.8 us
    ppermute x18, starting transfers between devices, exchange(): parts.append(lax.ppermute(block, axis, route))  25.3 us
    ppermute x18, waiting for transfers between devices, exchange(): parts.append(lax.ppermute(block, axis, route))  22.5 us
    all_to_all x1, starting transfers between devices, body(): lax.all_to_all(late, 'dp', 0, 0, tiled=True)  4.44 us
  transfers between devices with their start and end apart: 20, of which 6 were waited for; matrix products, arithmetic and copies ran while one was open for 1% of the time, Pallas kernels for 32%

profile of v1, /device:TPU:0, one launch (start us, length us, event | category | flops | bytes accessed | tf_op | source)
XLA Modules:
  0.0 115.5 jit_solution(13807675921028621473)
XLA Ops:
  0.7 14.5 %shard_map.339 = (bf16[20,512]{1,0:T(8,128)(2,1)}, bf16[20,2432]{1,0:T(8,128)(2,1)}, bf16[1080,768]{1,0:T(8,128)(2,1)}, f32[1080,128]{1,0:T(8,128)}, f32[240,108...) custom-call(s32[1,20]{1,0:T(1,128)} %bitcast.11, ...), custom_call_target="tpu_custom_call" | custom-call | flops 1000000000 | bytes 20000000 | tf_op jit(solution)/shard_map/pallas_call | solution.py:871
  15.2 0.0 copy-start.9
  15.2 0.0 copy-start.8
  15.2 0.0 copy-start.11
  15.2 5.1 %collective-permute-start.2 = (bf16[20,512]{1,0:T(8,128)(2,1)}, bf16[20,512]{1,0:T(8,128)(2,1)S(1)}, u32[]{:S(2)}, u32[]{:S(2)}) collective-permute-start(bf16[20,512]{1,0:T(8,128)(2,1)} %get-tuple-element.82), channel_id=1, source_target_pairs={{0,12},{1,13},{2,14},{3,15},{4,8},{5,9},{6,10},{7,11},{8,4},{9,5},... | collective-permute-start | bytes 61448 | tf_op jit(solution)/shard_map/ppermute | solution.py:861
  20.3 0.1 collective-permute-start.5
  20.4 0.9 collective-permute-start.4
  21.4 3.4 %collective-permute-start.3 = (bf16[20,2432]{1,0:T(8,128)(2,1)}, bf16[20,2432]{1,0:T(8,128)(2,1)S(1)}, u32[]{:S(2)}, u32[]{:S(2)}) collective-permute-start(bf16[20,2432]{1,0:T(8,128)(2,1)} %get-tuple-element.101), channel_id=1, source_target_pairs={{0,4},{1,5},{2,6},{3,7},{4,0},{5,1},{6,2},{7,3},{8,12},{9,13},{10,... | collective-permute-start | bytes 291848 | tf_op jit(solution)/shard_map/ppermute | solution.py:861
  24.7 0.0 collective-permute-start.1
  24.7 0.0 collective-permute-done.2
  24.7 0.6 collective-permute-start
  25.4 3.4 %shard_map.340 = (bf16[768,256]{1,0:T(8,128)(2,1)}, f32[240,768]{1,0:T(8,128)}) custom-call(f32[1,768]{1,0:T(1,128)} %refs_5_.1, f32[1,768]{1,0:T(1,128)} %refs_6_.1, bf16[1080,768]{1,0:T(8,128)(2,1)} %get-tuple-element.78.hat_ref.hat_hbm, f32[240,1080]{1,0:T(8,128)} %get-tuple-element.79.probs_ref.probs_hbm), custom_call_target="tpu_custom_call" | custom-call | flops 1000000000 | bytes 5000000 | tf_op jit(solution)/shard_map/pallas_call | solution.py:871
  28.8 4.3 %collective-permute-done.1 = bf16[20,512]{1,0:T(8,128)(2,1)S(1)} collective-permute-done((bf16[20,512]{1,0:T(8,128)(2,1)}, bf16[20,512]{1,0:T(8,128)(2,1)S(1)}, u32[]{:S(2)}, u32[]{:S(2)}) %collective-permute-start.1) | collective-permute-done | bytes 20512 | tf_op jit(solution)/shard_map/ppermute | solution.py:861
  33.1 0.0 collective-permute-done.3
  33.2 2.5 %collective-permute-start.8 = (bf16[80,512]{1,0:T(8,128)(2,1)S(1)}, bf16[80,512]{1,0:T(8,128)(2,1)S(1)}, u32[]{:S(2)}, u32[]{:S(2)}) collective-permute-start(bf16[80,512]{1,0:T(8,128)(2,1)S(1)} %pad_maximum_fusion.2), channel_id=1, source_target_pairs={{0,3},{1,2},{2,1},{3,0},{4,7},{5,6},{6,5},{7,4},{8,11},{9,10},{10,... | collective-permute-start | bytes 245768 | tf_op jit(solution)/shard_map/ppermute | solution.py:861
  35.7 0.5 collective-permute-start.7
  36.2 0.5 collective-permute-start.6
  36.7 2.4 %collective-permute-done.8 = bf16[80,512]{1,0:T(8,128)(2,1)S(1)} collective-permute-done((bf16[80,512]{1,0:T(8,128)(2,1)S(1)}, bf16[80,512]{1,0:T(8,128)(2,1)S(1)}, u32[]{:S(2)}, u32[]{:S(2)}) %collective-permute-start.8) | collective-permute-done | bytes 81952 | tf_op jit(solution)/shard_map/ppermute | solution.py:861
  39.2 1.0 collective-permute-done.7
  40.1 0.5 collective-permute-done.6
  40.6 0.3 concatenate.14.own_rel
  40.9 0.1 collective-permute-start.9
  41.0 0.1 pad_maximum_fusion.refs_0_
  41.1 1.6 %collective-permute-start.12 = (bf16[80,2432]{1,0:T(8,128)(2,1)S(1)}, bf16[80,2432]{1,0:T(8,128)(2,1)S(1)}, u32[]{:S(2)}, u32[]{:S(2)}) collective-permute-start(bf16[80,2432]{1,0:T(8,128)(2,1)S(1)} %pad_maximum_fusion.refs_0_), channel_id=1, source_target_pairs={{0,3},{1,2},{2,1},{3,0},{4,7},{5,6},{6,5},{7,4},{8,11},{9,10},{10,... | collective-permute-start | bytes 1167368 | tf_op jit(solution)/shard_map/ppermute | solution.py:861
  42.7 0.6 collective-permute-start.11
  43.3 1.4 %collective-permute-start.10 = (bf16[80,2432]{1,0:T(8,128)(2,1)S(1)}, bf16[80,2432]{1,0:T(8,128)(2,1)S(1)}, u32[]{:S(2)}, u32[]{:S(2)}) collective-permute-start(bf16[80,2432]{1,0:T(8,128)(2,1)S(1)} %pad_maximum_fusion.refs_0_), channel_id=1, source_target_pairs={{0,1},{1,0},{2,3},{3,2},{4,5},{5,4},{6,7},{7,6},{8,9},{9,8},{10,11... | collective-permute-start | bytes 1167368 | tf_op jit(solution)/shard_map/ppermute | solution.py:861
  46.0 0.6 reshape.55.flags_ref
  46.6 0.0 collective-permute-done.9.other_rel
  46.6 0.7 copy-done.6
  47.3 15.6 %shard_map.341 = (f32[1,1]{1,0:T(1,128)}, f32[1,1]{1,0:T(1,128)}, f32[1,1]{1,0:T(1,128)}, f32[320,512]{1,0:T(8,128)}, bf16[768,512]{1,0:T(8,128)(2,1)}, /*index=...) custom-call(bf16[320,512]{1,0:T(8,128)(2,1)} %copy-done.1, ...), custom_call_target="tpu_custom_call" | custom-call | flops 1000000000 | bytes 20000000 | tf_op jit(solution)/shard_map/pallas_call | solution.py:871
  63.0 0.0 collective-permute-done.12.refs_3_
  63.0 0.0 copy-start.5
  63.0 4.4 %all-to-all-start = ((bf16[16,48,512]{2,1,0:T(8,128)(2,1)}), bf16[16,48,512]{2,1,0:T(8,128)(2,1)S(1)}, u32[]{:S(2)}, u32[]{:S(2)}) async-start(bf16[16,48,512]{2,1,0:T(8,128)(2,1)} %bitcast.10), calls=%async_computation | async-start | bytes 1572864 | tf_op jit(solution)/shard_map/all_to_all | solution.py:1079
  67.5 3.6 %collective-permute-start.15 = (bf16[20,1536]{1,0:T(8,128)(2,1)}, bf16[20,1536]{1,0:T(8,128)(2,1)S(1)}, u32[]{:S(2)}, u32[]{:S(2)}) collective-permute-start(bf16[20,1536]{1,0:T(8,128)(2,1)} %get-tuple-element.107), channel_id=1, source_target_pairs={{0,12},{1,13},{2,14},{3,15},{4,8},{5,9},{6,10},{7,11},{8,4},{9,5},... | collective-permute-start | bytes 184328 | tf_op jit(solution)/shard_map/ppermute | solution.py:861
  71.0 0.9 collective-permute-start.13
  71.9 7.3 %shard_map.342 = f32[1,1080,768]{2,1,0:T(8,128)} custom-call(s32[1,20]{1,0:T(1,128)} %bitcast.12, f32[1,768]{1,0:T(1,128)} %refs_5_.1, bf16[1080,768]{1,0:T(8,128)(2,1)} %get-tuple-element.78.hat_ref.hat_hbm, f32[1080,128]{1,0:T(8,128)} %get-tuple-element.96.inv_hbm, f32[240,1080]{1,0:T(8,128)} %get-tuple-element.79.probs_ref.probs_hbm, ...), custom_call_target="tpu_custom_call" | custom-call | flops 2000000000 | bytes 10000000 | tf_op jit(solution)/shard_map/pallas_call | solution.py:871
  79.2 7.8 %collective-permute-done.15 = bf16[20,1536]{1,0:T(8,128)(2,1)S(1)} collective-permute-done((bf16[20,1536]{1,0:T(8,128)(2,1)}, bf16[20,1536]{1,0:T(8,128)(2,1)S(1)}, u32[]{:S(2)}, u32[]{:S(2)}) %collective-permute-start.15) | collective-permute-done | bytes 61472 | tf_op jit(solution)/shard_map/ppermute | solution.py:861
  87.0 6.4 %collective-permute-done.14 = bf16[20,1536]{1,0:T(8,128)(2,1)S(1)} collective-permute-done((bf16[20,1536]{1,0:T(8,128)(2,1)}, bf16[20,1536]{1,0:T(8,128)(2,1)S(1)}, u32[]{:S(2)}, u32[]{:S(2)}) %collective-permute-start.14) | collective-permute-done | bytes 61472 | tf_op jit(solution)/shard_map/ppermute | solution.py:861
  93.5 0.1 pad_maximum_fusion.1.refs_0_
  93.5 2.4 %collective-permute-start.18 = (bf16[80,1536]{1,0:T(8,128)(2,1)S(1)}, bf16[80,1536]{1,0:T(8,128)(2,1)S(1)}, u32[]{:S(2)}, u32[]{:S(2)}) collective-permute-start(bf16[80,1536]{1,0:T(8,128)(2,1)S(1)} %pad_maximum_fusion.1.refs_0_), channel_id=1, source_target_pairs={{0,3},{1,2},{2,1},{3,0},{4,7},{5,6},{6,5},{7,4},{8,11},{9,10},{10,... | collective-permute-start | bytes 737288 | tf_op jit(solution)/shard_map/ppermute | solution.py:861
  96.0 0.6 collective-permute-start.17
  96.5 0.6 collective-permute-start.16
  97.1 10.4 %shard_map.343 = (bf16[320,48]{1,0:T(8,128)(2,1)}, bf16[320,768]{1,0:T(8,128)(2,1)}, bf16[320,48]{1,0:T(8,128)(2,1)}, f32[1,48,512]{2,1,0:T(8,128)}, f32[1,192,7...) custom-call(bf16[80,2432]{1,0:T(8,128)(2,1)} %copy-done, ...), custom_call_target="tpu_custom_call" | custom-call | flops 3000000000 | bytes 10000000 | tf_op jit(solution)/shard_map/pallas_call | solution.py:871
  107.6 0.6 copy-done.12
  108.2 0.1 copy-done.13
  108.4 0.1 copy-done.14
  108.4 0.3 copy-done.2
  108.7 6.5 %shard_map.344 = (f32[1,3,48,768]{3,2,1,0:T(8,128)}, f32[1,48,768]{2,1,0:T(8,128)}, f32[1,48]{1,0:T(1,128)}, f32[1,48]{1,0:T(1,128)}, f32[1,48]{1,0:T(1,128)}, /...) custom-call(bf16[80,1536]{1,0:T(8,128)(2,1)} %copy-done.7, bf16[80,1536]{1,0:T(8,128)(2,1)} %copy-done.14, ...), custom_call_target="tpu_custom_call" | custom-call | flops 1000000000 | bytes 10000000 | tf_op jit(solution)/shard_map/pallas_call | solution.py:871
  (33 shorter events, 0.1 us)
Async XLA Ops:
  15.2 17.9 %copy-start.9 = (bf16[20,512]{1,0:T(8,128)(2,1)S(1)}, bf16[20,512]{1,0:T(8,128)(2,1)}, u32[]{:S(2)}) copy-start(bf16[20,512]{1,0:T(8,128)(2,1)} %get-tuple-element.82) | copy-start | bytes 61444
  15.2 25.8 %copy-start.8 = (bf16[20,2432]{1,0:T(8,128)(2,1)S(1)}, bf16[20,2432]{1,0:T(8,128)(2,1)}, u32[]{:S(2)}) copy-start(bf16[20,2432]{1,0:T(8,128)(2,1)} %get-tuple-element.101) | copy-start | bytes 291844
  15.2 30.8 %copy-start.11 = (s32[320]{0:T(512)S(1)}, s32[320]{0:T(512)}, u32[]{:S(2)}) copy-start(s32[320]{0:T(512)} %param.23) | copy-start | bytes 3844
  15.2 9.5 %collective-permute-start.2 = (bf16[20,512]{1,0:T(8,128)(2,1)}, bf16[20,512]{1,0:T(8,128)(2,1)S(1)}, u32[]{:S(2)}, u32[]{:S(2)}) collective-permute-start(bf16[20,512]{1,0:T(8,128)(2,1)} %get-tuple-element.82), channel_id=1, source_target_pairs={{0,12},{1,13},{2,14},{3,15},{4,8},{5,9},{6,10},{7,11},{8,4},{9,5},... | collective-permute-start | bytes 61448 | tf_op jit(solution)/shard_map/ppermute | solution.py:861
  20.3 12.8 %collective-permute-start.5 = (bf16[20,2432]{1,0:T(8,128)(2,1)}, bf16[20,2432]{1,0:T(8,128)(2,1)S(1)}, u32[]{:S(2)}, u32[]{:S(2)}) collective-permute-start(bf16[20,2432]{1,0:T(8,128)(2,1)} %get-tuple-element.101), channel_id=1, source_target_pairs={{0,12},{1,13},{2,14},{3,15},{4,8},{5,9},{6,10},{7,11},{8,4},{9,5},... | collective-permute-start | bytes 291848 | tf_op jit(solution)/shard_map/ppermute | solution.py:861
  20.4 12.7 %collective-permute-start.4 = (bf16[20,2432]{1,0:T(8,128)(2,1)}, bf16[20,2432]{1,0:T(8,128)(2,1)S(1)}, u32[]{:S(2)}, u32[]{:S(2)}) collective-permute-start(bf16[20,2432]{1,0:T(8,128)(2,1)} %get-tuple-element.101), channel_id=1, source_target_pairs={{0,8},{1,9},{2,10},{3,11},{4,12},{5,13},{6,14},{7,15},{8,0},{9,1},... | collective-permute-start | bytes 291848 | tf_op jit(solution)/shard_map/ppermute | solution.py:861
  21.4 11.8 %collective-permute-start.3 = (bf16[20,2432]{1,0:T(8,128)(2,1)}, bf16[20,2432]{1,0:T(8,128)(2,1)S(1)}, u32[]{:S(2)}, u32[]{:S(2)}) collective-permute-start(bf16[20,2432]{1,0:T(8,128)(2,1)} %get-tuple-element.101), channel_id=1, source_target_pairs={{0,4},{1,5},{2,6},{3,7},{4,0},{5,1},{6,2},{7,3},{8,12},{9,13},{10,... | collective-permute-start | bytes 291848 | tf_op jit(solution)/shard_map/ppermute | solution.py:861
  24.7 8.4 %collective-permute-start.1 = (bf16[20,512]{1,0:T(8,128)(2,1)}, bf16[20,512]{1,0:T(8,128)(2,1)S(1)}, u32[]{:S(2)}, u32[]{:S(2)}) collective-permute-start(bf16[20,512]{1,0:T(8,128)(2,1)} %get-tuple-element.82), channel_id=1, source_target_pairs={{0,8},{1,9},{2,10},{3,11},{4,12},{5,13},{6,14},{7,15},{8,0},{9,1},... | collective-permute-start | bytes 61448 | tf_op jit(solution)/shard_map/ppermute | solution.py:861
  24.7 8.4 %collective-permute-start = (bf16[20,512]{1,0:T(8,128)(2,1)}, bf16[20,512]{1,0:T(8,128)(2,1)S(1)}, u32[]{:S(2)}, u32[]{:S(2)}) collective-permute-start(bf16[20,512]{1,0:T(8,128)(2,1)} %get-tuple-element.82), channel_id=1, source_target_pairs={{0,4},{1,5},{2,6},{3,7},{4,0},{5,1},{6,2},{7,3},{8,12},{9,13},{10,... | collective-permute-start | bytes 61448 | tf_op jit(solution)/shard_map/ppermute | solution.py:861
  33.2 6.0 %collective-permute-start.8 = (bf16[80,512]{1,0:T(8,128)(2,1)S(1)}, bf16[80,512]{1,0:T(8,128)(2,1)S(1)}, u32[]{:S(2)}, u32[]{:S(2)}) collective-permute-start(bf16[80,512]{1,0:T(8,128)(2,1)S(1)} %pad_maximum_fusion.2), channel_id=1, source_target_pairs={{0,3},{1,2},{2,1},{3,0},{4,7},{5,6},{6,5},{7,4},{8,11},{9,10},{10,... | collective-permute-start | bytes 245768 | tf_op jit(solution)/shard_map/ppermute | solution.py:861
  35.7 4.4 %collective-permute-start.7 = (bf16[80,512]{1,0:T(8,128)(2,1)S(1)}, bf16[80,512]{1,0:T(8,128)(2,1)S(1)}, u32[]{:S(2)}, u32[]{:S(2)}) collective-permute-start(bf16[80,512]{1,0:T(8,128)(2,1)S(1)} %pad_maximum_fusion.2), channel_id=1, source_target_pairs={{0,2},{1,3},{2,0},{3,1},{4,6},{5,7},{6,4},{7,5},{8,10},{9,11},{10,... | collective-permute-start | bytes 245768 | tf_op jit(solution)/shard_map/ppermute | solution.py:861
  36.2 4.4 %collective-permute-start.6 = (bf16[80,512]{1,0:T(8,128)(2,1)S(1)}, bf16[80,512]{1,0:T(8,128)(2,1)S(1)}, u32[]{:S(2)}, u32[]{:S(2)}) collective-permute-start(bf16[80,512]{1,0:T(8,128)(2,1)S(1)} %pad_maximum_fusion.2), channel_id=1, source_target_pairs={{0,1},{1,0},{2,3},{3,2},{4,5},{5,4},{6,7},{7,6},{8,9},{9,8},{10,11... | collective-permute-start | bytes 245768 | tf_op jit(solution)/shard_map/ppermute | solution.py:861
  40.9 5.7 %copy-start.1 = (bf16[320,512]{1,0:T(8,128)(2,1)}, bf16[320,512]{1,0:T(8,128)(2,1)S(1)}, u32[]{:S(2)}) copy-start(bf16[320,512]{1,0:T(8,128)(2,1)S(1)} %concatenate.14.own_rel) | copy-start | bytes 983044
  40.9 5.7 %collective-permute-start.9 = (bf16[320,512]{1,0:T(8,128)(2,1)S(1)}, bf16[320,512]{1,0:T(8,128)(2,1)S(1)}, u32[]{:S(2)}, u32[]{:S(2)}) collective-permute-start(bf16[320,512]{1,0:T(8,128)(2,1)S(1)} %concatenate.14.own_rel), channel_id=1, source_target_pairs={{0,16},{16,0},{1,17},{17,1},{2,18},{18,2},{3,19},{19,3},{4,20},{20... | collective-permute-start | bytes 983048 | tf_op jit(solution)/shard_map/ppermute | solution.py:1010
  41.1 21.8 %copy-start = (bf16[80,2432]{1,0:T(8,128)(2,1)}, bf16[80,2432]{1,0:T(8,128)(2,1)S(1)}, u32[]{:S(2)}) copy-start(bf16[80,2432]{1,0:T(8,128)(2,1)S(1)} %pad_maximum_fusion.refs_0_) | copy-start | bytes 1167364
  41.1 21.8 %collective-permute-start.12 = (bf16[80,2432]{1,0:T(8,128)(2,1)S(1)}, bf16[80,2432]{1,0:T(8,128)(2,1)S(1)}, u32[]{:S(2)}, u32[]{:S(2)}) collective-permute-start(bf16[80,2432]{1,0:T(8,128)(2,1)S(1)} %pad_maximum_fusion.refs_0_), channel_id=1, source_target_pairs={{0,3},{1,2},{2,1},{3,0},{4,7},{5,6},{6,5},{7,4},{8,11},{9,10},{10,... | collective-permute-start | bytes 1167368 | tf_op jit(solution)/shard_map/ppermute | solution.py:861
  42.7 20.3 %collective-permute-start.11 = (bf16[80,2432]{1,0:T(8,128)(2,1)S(1)}, bf16[80,2432]{1,0:T(8,128)(2,1)S(1)}, u32[]{:S(2)}, u32[]{:S(2)}) collective-permute-start(bf16[80,2432]{1,0:T(8,128)(2,1)S(1)} %pad_maximum_fusion.refs_0_), channel_id=1, source_target_pairs={{0,2},{1,3},{2,0},{3,1},{4,6},{5,7},{6,4},{7,5},{8,10},{9,11},{10,... | collective-permute-start | bytes 1167368 | tf_op jit(solution)/shard_map/ppermute | solution.py:861
  43.3 19.7 %collective-permute-start.10 = (bf16[80,2432]{1,0:T(8,128)(2,1)S(1)}, bf16[80,2432]{1,0:T(8,128)(2,1)S(1)}, u32[]{:S(2)}, u32[]{:S(2)}) collective-permute-start(bf16[80,2432]{1,0:T(8,128)(2,1)S(1)} %pad_maximum_fusion.refs_0_), channel_id=1, source_target_pairs={{0,1},{1,0},{2,3},{3,2},{4,5},{5,4},{6,7},{7,6},{8,9},{9,8},{10,11... | collective-permute-start | bytes 1167368 | tf_op jit(solution)/shard_map/ppermute | solution.py:861
  46.6 0.7 copy-start.6
  63.0 16.2 %copy-start.3 = (bf16[80,2432]{1,0:T(8,128)(2,1)}, bf16[80,2432]{1,0:T(8,128)(2,1)S(1)}, u32[]{:S(2)}) copy-start(bf16[80,2432]{1,0:T(8,128)(2,1)S(1)} %collective-permute-done.12.refs_3_) | copy-start | bytes 1167364
  63.0 16.2 %copy-start.4 = (bf16[80,2432]{1,0:T(8,128)(2,1)}, bf16[80,2432]{1,0:T(8,128)(2,1)S(1)}, u32[]{:S(2)}) copy-start(bf16[80,2432]{1,0:T(8,128)(2,1)S(1)} %collective-permute-done.11.refs_2_) | copy-start | bytes 1167364
  63.0 16.2 %copy-start.5 = (bf16[80,2432]{1,0:T(8,128)(2,1)}, bf16[80,2432]{1,0:T(8,128)(2,1)S(1)}, u32[]{:S(2)}) copy-start(bf16[80,2432]{1,0:T(8,128)(2,1)S(1)} %collective-permute-done.10.refs_1_) | copy-start | bytes 1167364
  63.0 44.6 %all-to-all-start = ((bf16[16,48,512]{2,1,0:T(8,128)(2,1)}), bf16[16,48,512]{2,1,0:T(8,128)(2,1)S(1)}, u32[]{:S(2)}, u32[]{:S(2)}) async-start(bf16[16,48,512]{2,1,0:T(8,128)(2,1)} %bitcast.10), calls=%async_computation | async-start | bytes 1572864 | tf_op jit(solution)/shard_map/all_to_all | solution.py:1079
  67.5 19.5 %collective-permute-start.15 = (bf16[20,1536]{1,0:T(8,128)(2,1)}, bf16[20,1536]{1,0:T(8,128)(2,1)S(1)}, u32[]{:S(2)}, u32[]{:S(2)}) collective-permute-start(bf16[20,1536]{1,0:T(8,128)(2,1)} %get-tuple-element.107), channel_id=1, source_target_pairs={{0,12},{1,13},{2,14},{3,15},{4,8},{5,9},{6,10},{7,11},{8,4},{9,5},... | collective-permute-start | bytes 184328 | tf_op jit(solution)/shard_map/ppermute | solution.py:861
  71.0 22.4 %collective-permute-start.14 = (bf16[20,1536]{1,0:T(8,128)(2,1)}, bf16[20,1536]{1,0:T(8,128)(2,1)S(1)}, u32[]{:S(2)}, u32[]{:S(2)}) collective-permute-start(bf16[20,1536]{1,0:T(8,128)(2,1)} %get-tuple-element.107), channel_id=1, source_target_pairs={{0,8},{1,9},{2,10},{3,11},{4,12},{5,13},{6,14},{7,15},{8,0},{9,1},... | collective-permute-start | bytes 184328 | tf_op jit(solution)/shard_map/ppermute | solution.py:861
  71.0 22.4 %collective-permute-start.13 = (bf16[20,1536]{1,0:T(8,128)(2,1)}, bf16[20,1536]{1,0:T(8,128)(2,1)S(1)}, u32[]{:S(2)}, u32[]{:S(2)}) collective-permute-start(bf16[20,1536]{1,0:T(8,128)(2,1)} %get-tuple-element.107), channel_id=1, source_target_pairs={{0,4},{1,5},{2,6},{3,7},{4,0},{5,1},{6,2},{7,3},{8,12},{9,13},{10,... | collective-permute-start | bytes 184328 | tf_op jit(solution)/shard_map/ppermute | solution.py:861
  71.9 21.5 %copy-start.10 = (bf16[20,1536]{1,0:T(8,128)(2,1)S(1)}, bf16[20,1536]{1,0:T(8,128)(2,1)}, u32[]{:S(2)}) copy-start(bf16[20,1536]{1,0:T(8,128)(2,1)} %get-tuple-element.107) | copy-start | bytes 184324
  93.5 14.0 %copy-start.7 = (bf16[80,1536]{1,0:T(8,128)(2,1)}, bf16[80,1536]{1,0:T(8,128)(2,1)S(1)}, u32[]{:S(2)}) copy-start(bf16[80,1536]{1,0:T(8,128)(2,1)S(1)} %pad_maximum_fusion.1.refs_0_) | copy-start | bytes 737284
  93.5 14.0 %collective-permute-start.18 = (bf16[80,1536]{1,0:T(8,128)(2,1)S(1)}, bf16[80,1536]{1,0:T(8,128)(2,1)S(1)}, u32[]{:S(2)}, u32[]{:S(2)}) collective-permute-start(bf16[80,1536]{1,0:T(8,128)(2,1)S(1)} %pad_maximum_fusion.1.refs_0_), channel_id=1, source_target_pairs={{0,3},{1,2},{2,1},{3,0},{4,7},{5,6},{6,5},{7,4},{8,11},{9,10},{10,... | collective-permute-start | bytes 737288 | tf_op jit(solution)/shard_map/ppermute | solution.py:861
  96.0 11.6 %collective-permute-start.17 = (bf16[80,1536]{1,0:T(8,128)(2,1)S(1)}, bf16[80,1536]{1,0:T(8,128)(2,1)S(1)}, u32[]{:S(2)}, u32[]{:S(2)}) collective-permute-start(bf16[80,1536]{1,0:T(8,128)(2,1)S(1)} %pad_maximum_fusion.1.refs_0_), channel_id=1, source_target_pairs={{0,2},{1,3},{2,0},{3,1},{4,6},{5,7},{6,4},{7,5},{8,10},{9,11},{10,... | collective-permute-start | bytes 737288 | tf_op jit(solution)/shard_map/ppermute | solution.py:861
  96.5 11.1 %collective-permute-start.16 = (bf16[80,1536]{1,0:T(8,128)(2,1)S(1)}, bf16[80,1536]{1,0:T(8,128)(2,1)S(1)}, u32[]{:S(2)}, u32[]{:S(2)}) collective-permute-start(bf16[80,1536]{1,0:T(8,128)(2,1)S(1)} %pad_maximum_fusion.1.refs_0_), channel_id=1, source_target_pairs={{0,1},{1,0},{2,3},{3,2},{4,5},{5,4},{6,7},{7,6},{8,9},{9,8},{10,11... | collective-permute-start | bytes 737288 | tf_op jit(solution)/shard_map/ppermute | solution.py:861
  107.6 0.7 copy-start.12
  107.6 0.8 copy-start.13
  107.6 0.9 copy-start.14
  107.6 1.1 copy-start.2
